TPU v7x, 256 devices: a whole 4x4x8 slice. The times are simulated.
256 devices in a mesh: gx: 4 (over x), gy: 8 (over y, core), gz: 8 (over z).
Axes of the slice: x: 4, y: 4, z: 8, core: 2. Of those that a mesh axis runs over, the one named last changes fastest.
Arguments:
- velocity: float32 [3, 32, 256, 1024], P(None, 'gx', 'gy', 'gz'), may hold values from -6 to 6
- inverse_coef: float32 [32, 256, 1024], P('gx', 'gy', 'gz'), may hold values from 0.3 to 3
- enthalpy: float32 [32, 256, 1024], P('gx', 'gy', 'gz'), may hold values from -6 to 6
- void: float32 [32, 256, 1024], P('gx', 'gy', 'gz'), may hold values from 0.05 to 0.7
- wall_cells: int32 [4096, 128], P(('gx', 'gy', 'gz')), may hold values from 0 to 32767, as said below
- wall_normal: int32 [4096, 128], P(('gx', 'gy', 'gz')), may hold values from 0 to 5
- wall_flag: int32 [4096, 128], P(('gx', 'gy', 'gz')), may hold values from 0 to 2, as said below
Outputs:
- velocity_new: float32 [3, 32, 256, 1024], P(None, 'gx', 'gy', 'gz')
- pressure: float32 [32, 256, 1024], P('gx', 'gy', 'gz')
- enthalpy_new: float32 [32, 256, 1024], P('gx', 'gy', 'gz')
Inputs may be any that keep to these rules, and one draw needn't show every extreme that they name: `wall_cells`: the indices within the 16 tile rows of one device are all distinct. `wall_flag`: on each device the live tiles come first, 1 to 16 of them, every slot of a live tile is 1 or 2 and every slot of the others 0; some device has all 16 tiles live.
All inputs are finite; a program needn't handle non-finite values.
Results may differ from a plain program's by a relative error of at most 0.0001.
Values sent between devices are 32-bit elements; how exact they have to be, the bound alone decides.
A program may use at most 128 MiB of HBM per device.

v0:
```python
import jax
import jax.numpy as jnp
from jax import lax
from jax.sharding import PartitionSpec as P

ITERS = 3


DIFFUSE = 0.1
HEATING = 0.5
LATENT = 2.0
EXPANSION = 1.5


def with_halo(x, sides, width):
    for axis, dim in sides:
        size, length = (lax.axis_size(axis), x.shape[dim])
        up = [(i, (i + 1) % size) for i in range(size - 1)]
        down = [(j, i) for i, j in up]
        last = lax.slice_in_dim(x, length - width, length, axis=dim)
        first = lax.slice_in_dim(x, 0, width, axis=dim)
        before = lax.ppermute(last, axis, up)
        after = lax.ppermute(first, axis, down)
        x = jnp.concatenate([before, x, after], axis=dim)
    return x


def shifted(padded):
    return (
        padded[..., 2:, 1:-1, 1:-1],
        padded[..., :-2, 1:-1, 1:-1],
        padded[..., 1:-1, 2:, 1:-1],
        padded[..., 1:-1, :-2, 1:-1],
        padded[..., 1:-1, 1:-1, 2:],
        padded[..., 1:-1, 1:-1, :-2],
    )


def inner(padded):
    return padded[..., 1:-1, 1:-1, 1:-1]


def wall_flux(comps, void_cells, normal, flag):
    which = normal // 2
    select = (jnp.arange(3, dtype=jnp.int32)[:, None, None] == which[None]).astype(jnp.float32)
    parallel = jnp.sum(comps * comps * (1.0 - select), axis=0)
    speed = jnp.sqrt(parallel + 0.25)
    heat_level = flag.astype(jnp.float32)
    liquid = 1.0 - void_cells
    evap = 1.5 * void_cells * heat_level * heat_level
    total = liquid * speed * heat_level + 0.6 * liquid * heat_level * jnp.sqrt(heat_level) + evap
    return (total, evap / LATENT)


def balance_terms(stacked_pad, heat_source, mass_source):
    near_h = shifted(stacked_pad[3])
    centre_h = inner(stacked_pad[3])
    laplace = near_h[0] + near_h[1] + near_h[2] + near_h[3] + near_h[4] + near_h[5] - 6.0 * centre_h
    enthalpy_new = centre_h + DIFFUSE * laplace + HEATING * heat_source
    near_u = shifted(stacked_pad[0:3])
    diverge = 0.5 * (
        near_u[0][0] - near_u[1][0] + (near_u[2][1] - near_u[3][1]) + (near_u[4][2] - near_u[5][2])
    )
    imbalance = EXPANSION * mass_source - diverge
    return (enthalpy_new, imbalance)


def apply_operator(coef_pad, field_pad):
    centre_c = inner(coef_pad)
    centre_v = inner(field_pad)
    total = jnp.zeros(centre_v.shape, jnp.float32)
    for near_c, near_v in zip(shifted(coef_pad), shifted(field_pad)):
        total = total + 0.5 * (centre_c + near_c) * (centre_v - near_v)
    return total


def correct_velocity(velocity, coef, pressure_pad):
    near = shifted(pressure_pad)
    slope = jnp.stack(
        [0.5 * (near[0] - near[1]), 0.5 * (near[2] - near[3]), 0.5 * (near[4] - near[5])]
    )
    return velocity - coef[None] * slope


def spread_rims(field):
    return with_halo(field, (("gx", 0), ("gy", 1), ("gz", 2)), 1)


def squares(field):
    return lax.psum(jnp.sum(field * field), ("gx", "gy", "gz"))


def accumulate(pressure, alpha, direction_pad):
    return pressure + alpha * inner(direction_pad)


def shards(velocity, inverse_coef, enthalpy, void, wall_cells, wall_normal, wall_flag):
    cells = enthalpy.shape[0] * enthalpy.shape[1] * enthalpy.shape[2]
    comps = velocity.reshape(3, cells)[:, wall_cells]
    void_cells = void.reshape(cells)[wall_cells]
    heat, evap = wall_flux(comps, void_cells, wall_normal, wall_flag)
    sources = jnp.zeros((2, cells), jnp.float32)
    sources = sources.at[:, wall_cells.reshape(-1)].add(
        jnp.stack([heat.reshape(-1), evap.reshape(-1)])
    )
    sources = sources.reshape((2,) + enthalpy.shape)
    stacked = jnp.concatenate([velocity, enthalpy[None], inverse_coef[None]], axis=0)
    stacked_pad = with_halo(stacked, (("gx", 1), ("gy", 2), ("gz", 3)), 1)
    enthalpy_new, imbalance = balance_terms(stacked_pad, sources[0], sources[1])
    coef_pad = stacked_pad[4]
    pressure = jnp.zeros(imbalance.shape, jnp.float32)
    residual = imbalance
    direction = imbalance
    norm_now = squares(residual)
    for step in range(ITERS):
        direction_pad = spread_rims(direction)
        image = apply_operator(coef_pad, direction_pad)
        alpha = norm_now / lax.psum(jnp.sum(direction * image), ("gx", "gy", "gz"))
        pressure = accumulate(pressure, alpha, direction_pad)
        residual = residual - alpha * image
        norm_next = squares(residual)
        direction = residual + norm_next / norm_now * direction
        norm_now = norm_next
    pressure_pad = with_halo(pressure, (("gx", 0), ("gy", 1), ("gz", 2)), 1)
    velocity_new = correct_velocity(velocity, inverse_coef, pressure_pad)
    return (velocity_new, inner(pressure_pad), enthalpy_new)


def solution(mesh):
    in_specs = (
        P(None, "gx", "gy", "gz"),
        P("gx", "gy", "gz"),
        P("gx", "gy", "gz"),
        P("gx", "gy", "gz"),
        P(("gx", "gy", "gz"), None),
        P(("gx", "gy", "gz"), None),
        P(("gx", "gy", "gz"), None),
    )
    out_specs = (P(None, "gx", "gy", "gz"), P("gx", "gy", "gz"), P("gx", "gy", "gz"))
    return jax.shard_map(shards, mesh=mesh, in_specs=in_specs, out_specs=out_specs, check_vma=False)
```

profile of v0, /device:TPU:1, one launch (start us, length us, event | category | flops | bytes accessed | tf_op | source)
XLA Modules:
  0.0 600.8 jit_solution(7781071297566563430)
XLA Ops:
  1.6 3.9 collective-permute-start.1
  6.9 9.6 %copy.17 = f32[3,8,32,128]{0,3,2,1:T(8,128)} copy(f32[3,8,32,128]{3,2,1,0:T(8,128)} %param.7) | data formatting | bytes 786432 | tf_op args[0]
  16.5 11.2 %gather_fusion.1 = f32[2048,3]{1,0:T(8,128)S(1)} fusion(f32[3,32768]{0,1:T(8,128)} %bitcast.54, s32[2048]{0:T(1024)S(1)} %fusion.99), kind=kCustom, calls=%fused_computation.1 | custom fusion | bytes 57344 | tf_op jit(solution)/shard_map/gather | solution.py:99
  28.6 11.8 %gather_fusion = f32[2048]{0:T(1024)S(1)} fusion(f32[32768]{0:T(1024)S(1)} %bitcast.53, s32[2048]{0:T(1024)S(1)} %fusion.99), kind=kCustom, calls=%fused_computation | custom fusion | bytes 24576 | tf_op jit(solution)/shard_map/gather | solution.py:100
  40.4 4.0 collective-permute-start.3
  44.5 1.9 collective-permute-start.2
  46.5 3.2 collective-permute-done.2
  51.0 3.5 collective-permute-start.5
  56.3 18.2 %scatter_custom_fusion = f32[2,32768]{0,1:T(8,128)} fusion(s32[2048]{0:T(1024)S(1)} %bitcast.72, f32[2048,2]{1,0:T(8,128)S(1)} %copy.18, f32[]{:T(128)} %constant.12.clone.1), kind=kCustom, calls=%fused_computation.8 | custom fusion | flops 4096 | bytes 262148 | tf_op jit(solution)/shard_map/scatter-add | solution.py:103
  75.7 8.2 %copy.23 = f32[1,32768]{0,1:T(8,128)} copy(f32[1,32768]{1,0:T(1,128)S(1)} %bitcast.66) | data formatting | bytes 262144 | tf_op jit(solution)/shard_map/mul | solution.py:61
  83.9 22.2 %fusion = (f32[32768]{0:T(1024)S(1)}, f32[32768]{0:T(1024)S(1)}, f32[]{:T(128)}) fusion(f32[2,32768]{0,1:T(8,128)} %scatter_custom_fusion, f32[1,32768]{0,1:T(8,128)} %copy.23), kind=kLoop, calls=%fused_computation.4 | loop fusion | flops 163839 | bytes 655364 | tf_op jit(solution)/shard_map/mul | solution.py:59
  106.1 4.3 collective-permute-start.7
  111.7 3.2 collective-permute-done.6
  114.9 3.7 collective-permute-start.9
  118.5 1.9 collective-permute-start.8
  121.6 1.9 collective-permute-done.8
  124.9 5.0 collective-permute-start.11
  130.0 1.6 collective-permute-done.10
  131.6 1.8 collective-permute-done.11
  134.4 80.9 %all-reduce = (f32[]{:T(128)}, f32[]{:T(128)}) all-reduce(f32[]{:T(128)} %get-tuple-element.5, f32[]{:T(128)} %get-tuple-element.12), channel_id=1, replica_groups=mesh['gx'=4,'gy'=8,'gz'=8] {'gx','gy','gz'}, use_global_device_ids=true, to_apply=%region_3.4 | all-reduce | flops 2 | bytes 16 | tf_op jit(solution)/shard_map/psum | solution.py:90
  217.3 73.7 %psum.44 = f32[]{:T(128)} all-reduce(f32[]{:T(128)} %get-tuple-element.10), channel_id=1, replica_groups=mesh['gx'=4,'gy'=8,'gz'=8] {'gx','gy','gz'}, use_global_device_ids=true, to_apply=%region_7.8 | all-reduce | flops 1 | bytes 8 | tf_op jit(solution)/shard_map/psum | solution.py:90
  292.4 2.4 collective-permute-start.13
  296.1 3.2 collective-permute-done.12
  299.2 3.3 collective-permute-start.15
  302.5 2.0 collective-permute-start.14
  304.6 2.9 collective-permute-done.14
  308.9 4.0 collective-permute-start.17
  312.9 2.1 collective-permute-done.16
  315.0 1.8 collective-permute-done.17
  317.7 76.5 %psum.45 = f32[]{:T(128)} all-reduce(f32[]{:T(128)} %get-tuple-element.8), channel_id=1, replica_groups=mesh['gx'=4,'gy'=8,'gz'=8] {'gx','gy','gz'}, use_global_device_ids=true, to_apply=%region_9.10 | all-reduce | flops 1 | bytes 8 | tf_op jit(solution)/shard_map/psum | solution.py:118
  396.2 74.4 %psum.46 = f32[]{:T(128)} all-reduce(f32[]{:T(128)} %multiply_reduce_fusion.2), channel_id=1, replica_groups=mesh['gx'=4,'gy'=8,'gz'=8] {'gx','gy','gz'}, use_global_device_ids=true, to_apply=%region_11.12 | all-reduce | flops 1 | bytes 8 | tf_op jit(solution)/shard_map/psum | solution.py:90
  472.0 2.5 collective-permute-start.19
  475.8 3.2 collective-permute-done.18
  478.9 3.3 collective-permute-start.21
  482.2 2.0 collective-permute-start.20
  484.3 2.9 collective-permute-done.20
  488.6 4.0 collective-permute-start.23
  492.6 2.1 collective-permute-done.22
  494.7 1.8 collective-permute-done.23
  497.5 76.5 %psum.47 = f32[]{:T(128)} all-reduce(f32[]{:T(128)} %fusion.38), channel_id=1, replica_groups=mesh['gx'=4,'gy'=8,'gz'=8] {'gx','gy','gz'}, use_global_device_ids=true, to_apply=%region_13.14 | all-reduce | flops 1 | bytes 8 | tf_op jit(solution)/shard_map/psum | solution.py:118
  575.4 1.3 collective-permute-start.25
  578.0 3.2 collective-permute-done.24
  581.2 4.4 collective-permute-start.27
  585.7 1.9 collective-permute-start.26
  588.5 2.1 collective-permute-done.26
  592.0 4.0 collective-permute-start.29
  596.1 1.9 collective-permute-done.28
  598.0 1.8 collective-permute-done.29
  (89 shorter events, 25.8 us)
Async XLA Ops:
  0.6 27.9 %copy-start = (f32[8,32,128]{2,1,0:T(8,128)S(1)}, f32[8,32,128]{2,1,0:T(8,128)}, u32[]{:S(2)}) copy-start(f32[8,32,128]{2,1,0:T(8,128)} %param.10) | copy-start | bytes 393220
  1.6 38.8 %collective-permute-start.1 = (f32[5,1,32,128]{3,2,1,0:T(8,128)S(1)}, f32[5,1,32,128]{3,2,1,0:T(8,128)S(1)}, u32[]{:S(2)}, u32[]{:S(2)}) collective-permute-start(f32[5,1,32,128]{3,2,1,0:T(8,128)S(1)} %get-tuple-element.20), channel_id=1, source_target_pairs={{0,64},{64,128},{128,192},{1,65},{65,129},{129,193},{2,66},{66,130... | collective-permute-start | bytes 245768 | tf_op jit(solution)/shard_map/ppermute | solution.py:22
  5.5 10.9 %copy-start.6 = (s32[16,128]{1,0:T(8,128)S(1)}, s32[16,128]{1,0:T(8,128)}, u32[]{:S(2)}) copy-start(s32[16,128]{1,0:T(8,128)} %param.11) | copy-start | bytes 24580
  5.6 10.9 %copy-start.8 = (s32[16,128]{1,0:T(8,128)S(1)}, s32[16,128]{1,0:T(8,128)}, u32[]{:S(2)}) copy-start(s32[16,128]{1,0:T(8,128)} %param.12) | copy-start | bytes 24580
  5.6 34.8 %collective-permute-start = (f32[5,1,32,128]{3,2,1,0:T(8,128)S(1)}, f32[5,1,32,128]{3,2,1,0:T(8,128)S(1)}, u32[]{:S(2)}, u32[]{:S(2)}) collective-permute-start(f32[5,1,32,128]{3,2,1,0:T(8,128)S(1)} %get-tuple-element.21), channel_id=1, source_target_pairs={{64,0},{128,64},{192,128},{65,1},{129,65},{193,129},{66,2},{130,66... | collective-permute-start | bytes 245768 | tf_op jit(solution)/shard_map/ppermute | solution.py:23
  28.5 11.9 %copy-start.2 = (f32[3,8,32,128]{3,2,1,0:T(8,128)S(1)}, f32[3,8,32,128]{3,2,1,0:T(8,128)}, u32[]{:S(2)}) copy-start(f32[3,8,32,128]{3,2,1,0:T(8,128)} %param.7) | copy-start | bytes 1179652
  28.5 11.9 %copy-start.3 = (f32[8,32,128]{2,1,0:T(8,128)S(1)}, f32[8,32,128]{2,1,0:T(8,128)}, u32[]{:S(2)}) copy-start(f32[8,32,128]{2,1,0:T(8,128)} %param.8) | copy-start | bytes 393220
  28.5 11.9 %copy-start.5 = (f32[8,32,128]{2,1,0:T(8,128)S(1)}, f32[8,32,128]{2,1,0:T(8,128)}, u32[]{:S(2)}) copy-start(f32[8,32,128]{2,1,0:T(8,128)} %param.9) | copy-start | bytes 393220
  28.5 17.9 %copy-start.7 = (s32[16,128]{1,0:T(8,128)S(1)}, s32[16,128]{1,0:T(8,128)}, u32[]{:S(2)}) copy-start(s32[16,128]{1,0:T(8,128)} %param.13) | copy-start | bytes 24580
  40.4 6.0 %collective-permute-start.3 = (f32[5,10,1,128]{3,2,1,0:T(1,128)S(1)}, f32[5,10,1,128]{3,2,1,0:T(1,128)S(1)}, u32[]{:S(2)}, u32[]{:S(2)}) collective-permute-start(f32[5,10,1,128]{3,2,1,0:T(1,128)S(1)} %get-tuple-element.18), channel_id=1, source_target_pairs={{0,8},{8,16},{16,24},{24,32},{32,40},{40,48},{48,56},{1,9},{9,17},... | collective-permute-start | bytes 76808 | tf_op jit(solution)/shard_map/ppermute | solution.py:22
  44.5 5.2 collective-permute-start.2
  51.0 24.0 %collective-permute-start.5 = (f32[5,10,34,1]{2,3,1,0:T(1,128)S(1)}, f32[5,10,34,1]{2,3,1,0:T(1,128)S(1)}, u32[]{:S(2)}, u32[]{:S(2)}) collective-permute-start(f32[5,10,34,1]{2,3,1,0:T(1,128)S(1)} %copy.21), channel_id=1, source_target_pairs={{0,1},{1,2},{2,3},{3,4},{4,5},{5,6},{6,7},{8,9},{9,10},{10,11},{11... | collective-permute-start | bytes 20408 | tf_op jit(solution)/shard_map/ppermute | solution.py:22
  54.6 19.9 %collective-permute-start.4 = (f32[5,10,34,1]{2,3,1,0:T(1,128)S(1)}, f32[5,10,34,1]{2,3,1,0:T(1,128)S(1)}, u32[]{:S(2)}, u32[]{:S(2)}) collective-permute-start(f32[5,10,34,1]{2,3,1,0:T(1,128)S(1)} %copy.19), channel_id=1, source_target_pairs={{1,0},{2,1},{3,2},{4,3},{5,4},{6,5},{7,6},{9,8},{10,9},{11,10},{12... | collective-permute-start | bytes 20408 | tf_op jit(solution)/shard_map/ppermute | solution.py:23
  106.1 5.6 collective-permute-start.7
  110.4 4.5 collective-permute-start.6
  114.9 6.7 %collective-permute-start.9 = (f32[10,1,128]{2,1,0:T(1,128)S(1)}, f32[10,1,128]{2,1,0:T(1,128)S(1)}, u32[]{:S(2)}, u32[]{:S(2)}) collective-permute-start(f32[10,1,128]{2,1,0:T(1,128)S(1)} %get-tuple-element.38), channel_id=1, source_target_pairs={{0,8},{8,16},{16,24},{24,32},{32,40},{40,48},{48,56},{1,9},{9,17},... | collective-permute-start | bytes 15368 | tf_op jit(solution)/shard_map/ppermute | solution.py:22
  118.5 4.9 collective-permute-start.8
  123.6 8.0 %collective-permute-start.10 = (f32[10,34,1]{2,1,0:T(8,128)S(1)}, f32[10,34,1]{2,1,0:T(8,128)S(1)}, u32[]{:S(2)}, u32[]{:S(2)}) collective-permute-start(f32[10,34,1]{2,1,0:T(8,128)S(1)} %get-tuple-element.28), channel_id=1, source_target_pairs={{1,0},{2,1},{3,2},{4,3},{5,4},{6,5},{7,6},{9,8},{10,9},{11,10},{12... | collective-permute-start | bytes 4088 | tf_op jit(solution)/shard_map/ppermute | solution.py:23
  124.9 8.5 %collective-permute-start.11 = (f32[10,34,1]{2,1,0:T(8,128)S(1)}, f32[10,34,1]{2,1,0:T(8,128)S(1)}, u32[]{:S(2)}, u32[]{:S(2)}) collective-permute-start(f32[10,34,1]{2,1,0:T(8,128)S(1)} %get-tuple-element.29), channel_id=1, source_target_pairs={{0,1},{1,2},{2,3},{3,4},{4,5},{5,6},{6,7},{8,9},{9,10},{10,11},{11... | collective-permute-start | bytes 4088 | tf_op jit(solution)/shard_map/ppermute | solution.py:22
  292.4 3.7 collective-permute-start.13
  294.7 4.5 collective-permute-start.12
  299.2 5.3 collective-permute-start.15
  302.5 4.9 collective-permute-start.14
  307.6 7.4 %collective-permute-start.16 = (f32[10,34,1]{2,1,0:T(8,128)S(1)}, f32[10,34,1]{2,1,0:T(8,128)S(1)}, u32[]{:S(2)}, u32[]{:S(2)}) collective-permute-start(f32[10,34,1]{2,1,0:T(8,128)S(1)} %get-tuple-element.26), channel_id=1, source_target_pairs={{1,0},{2,1},{3,2},{4,3},{5,4},{6,5},{7,6},{9,8},{10,9},{11,10},{12... | collective-permute-start | bytes 4088 | tf_op jit(solution)/shard_map/ppermute | solution.py:23
  308.9 7.8 %collective-permute-start.17 = (f32[10,34,1]{2,1,0:T(8,128)S(1)}, f32[10,34,1]{2,1,0:T(8,128)S(1)}, u32[]{:S(2)}, u32[]{:S(2)}) collective-permute-start(f32[10,34,1]{2,1,0:T(8,128)S(1)} %get-tuple-element.27), channel_id=1, source_target_pairs={{0,1},{1,2},{2,3},{3,4},{4,5},{5,6},{6,7},{8,9},{9,10},{10,11},{11... | collective-permute-start | bytes 4088 | tf_op jit(solution)/shard_map/ppermute | solution.py:22
  472.0 3.8 collective-permute-start.19
  474.4 4.5 collective-permute-start.18
  478.9 5.3 collective-permute-start.21
  482.2 4.9 collective-permute-start.20
  487.3 7.4 %collective-permute-start.22 = (f32[10,34,1]{2,1,0:T(8,128)S(1)}, f32[10,34,1]{2,1,0:T(8,128)S(1)}, u32[]{:S(2)}, u32[]{:S(2)}) collective-permute-start(f32[10,34,1]{2,1,0:T(8,128)S(1)} %get-tuple-element.24), channel_id=1, source_target_pairs={{1,0},{2,1},{3,2},{4,3},{5,4},{6,5},{7,6},{9,8},{10,9},{11,10},{12... | collective-permute-start | bytes 4088 | tf_op jit(solution)/shard_map/ppermute | solution.py:23
  488.6 7.8 %collective-permute-start.23 = (f32[10,34,1]{2,1,0:T(8,128)S(1)}, f32[10,34,1]{2,1,0:T(8,128)S(1)}, u32[]{:S(2)}, u32[]{:S(2)}) collective-permute-start(f32[10,34,1]{2,1,0:T(8,128)S(1)} %get-tuple-element.25), channel_id=1, source_target_pairs={{0,1},{1,2},{2,3},{3,4},{4,5},{5,6},{6,7},{8,9},{9,10},{10,11},{11... | collective-permute-start | bytes 4088 | tf_op jit(solution)/shard_map/ppermute | solution.py:22
  575.4 25.4 %copy-start.4 = (f32[8,32,128]{2,1,0:T(8,128)}, f32[8,32,128]{2,1,0:T(8,128)S(1)}, u32[]{:S(2)}) copy-start(f32[8,32,128]{2,1,0:T(8,128)S(1)} %multiply_add_fusion) | copy-start | bytes 393220
  575.4 2.6 collective-permute-start.25
  576.7 4.5 collective-permute-start.24
  581.2 7.3 %collective-permute-start.27 = (f32[10,1,128]{2,1,0:T(1,128)S(1)}, f32[10,1,128]{2,1,0:T(1,128)S(1)}, u32[]{:S(2)}, u32[]{:S(2)}) collective-permute-start(f32[10,1,128]{2,1,0:T(1,128)S(1)} %get-tuple-element.32), channel_id=1, source_target_pairs={{0,8},{8,16},{16,24},{24,32},{32,40},{40,48},{48,56},{1,9},{9,17},... | collective-permute-start | bytes 15368 | tf_op jit(solution)/shard_map/ppermute | solution.py:22
  585.7 4.9 collective-permute-start.26
  587.6 13.2 %copy-start.1 = (f32[8,32,128]{2,1,0:T(8,128)S(1)}, f32[8,32,128]{2,1,0:T(8,128)}, u32[]{:S(2)}) copy-start(f32[8,32,128]{2,1,0:T(8,128)} %param.10) | copy-start | bytes 393220
  590.7 7.3 %collective-permute-start.28 = (f32[10,34,1]{2,1,0:T(8,128)S(1)}, f32[10,34,1]{2,1,0:T(8,128)S(1)}, u32[]{:S(2)}, u32[]{:S(2)}) collective-permute-start(f32[10,34,1]{2,1,0:T(8,128)S(1)} %get-tuple-element.22), channel_id=1, source_target_pairs={{1,0},{2,1},{3,2},{4,3},{5,4},{6,5},{7,6},{9,8},{10,9},{11,10},{12... | collective-permute-start | bytes 4088 | tf_op jit(solution)/shard_map/ppermute | solution.py:23
  592.0 7.7 %collective-permute-start.29 = (f32[10,34,1]{2,1,0:T(8,128)S(1)}, f32[10,34,1]{2,1,0:T(8,128)S(1)}, u32[]{:S(2)}, u32[]{:S(2)}) collective-permute-start(f32[10,34,1]{2,1,0:T(8,128)S(1)} %get-tuple-element.23), channel_id=1, source_target_pairs={{0,1},{1,2},{2,3},{3,4},{4,5},{5,6},{6,7},{8,9},{9,10},{10,11},{11... | collective-permute-start | bytes 4088 | tf_op jit(solution)/shard_map/ppermute | solution.py:22
where the time goes:
time: 603 us; the launch traced here: 601 us
  blocking collectives  382 us (63%)
  starting transfers between devices  76.3 us (13%)
  other arithmetic  50.1 us (8%)
  local copies, waits for them, and re-layouts  43.9 us (7%)
  waiting for transfers between devices  40.4 us (7%)
  between operations  8.01 us (1%)
    psum x3, blocking collectives, squares(): return lax.psum(jnp.sum(field * field), ('gx', 'gy', 'gz'))  229 us
    psum x2, blocking collectives, shards(): alpha = norm_now / lax.psum(jnp.sum(direction * image), ('gx', 'gy', 'gz'))  153 us
    ppermute x15, starting transfers between devices, with_halo(): before = lax.ppermute(last, axis, up)  53.6 us
    ppermute x15, waiting for transfers between devices, with_halo(): after = lax.ppermute(first, axis, down)  33.4 us
    ppermute x15, starting transfers between devices, with_halo(): after = lax.ppermute(first, axis, down)  22.7 us
    mul x1, other arithmetic, balance_terms(): enthalpy_new = centre_h + DIFFUSE * laplace + HEATING * heat_source  22.2 us
    scatter-add x1, other arithmetic, shards(): sources.at[:, wall_cells.reshape(-1)]  18.2 us
  transfers between devices with their start and end apart: 30, of which 17 were waited for; matrix products, arithmetic and copies ran while one was open for 9% of the time, Pallas kernels for 0%

commit v1 on v0

v1 whole, which is shorter than its diff:
```python
import jax
import jax.numpy as jnp
from jax import lax
from jax.experimental import pallas as pl
from jax.experimental.pallas import tpu as pltpu
from jax.sharding import PartitionSpec as P

MESH = pl.DeviceIdType.MESH
NGX, NGY, NGZ = 4, 8, 8
BX, BY, BZ = 8, 32, 128
SLOTS = 16
DIFFUSE = 0.1
HEATING = 0.5
EXPANSION = 1.5
SCALE = 16.0
U0, H, C, U1, U2, W0, W1, W2 = range(8)
TZ_U2, TZ_H, TZ_C, TZ_W0, TZ_W1, TZ_W2 = range(6)
ROWS = slice(8, 40)
PIVOT_FLOOR = 1e-9


def two_sum(a, b):
    s = a + b
    t = s - a
    return s, (a - (s - t)) + (b - t)


def quick_sum(a, b):
    s = a + b
    return s, b - (s - a)


def split(a):
    t = 4097.0 * a
    high = t - (t - a)
    return high, a - high


def two_mul(a, b):
    p = a * b
    ah, al = split(a)
    bh, bl = split(b)
    return p, ((ah * bh - p) + ah * bl + al * bh) + al * bl


def df_sub(a, b):
    s, e = two_sum(a[0], -b[0])
    return quick_sum(s, e + (a[1] - b[1]))


def df_mul(a, b):
    p, e = two_mul(a[0], b[0])
    return quick_sum(p, e + (a[0] * b[1] + a[1] * b[0]))


def df_div(a, b):
    q = a[0] / b[0]
    p, e = two_mul(q, b[0])
    rest = ((a[0] - p) - e) + a[1] - q * b[1]
    return quick_sum(q, rest / b[0])


def solve_moments(m):
    l10 = df_div(m[2], m[1])
    l20 = df_div(m[3], m[1])
    d1 = df_sub(m[3], df_mul(l10, m[2]))
    e12 = df_sub(m[4], df_mul(l10, m[3]))
    y1 = df_sub(m[1], df_mul(l10, m[0]))
    y2 = df_sub(m[2], df_mul(l20, m[0]))
    d2 = df_sub(m[5], df_mul(l20, m[3]))
    ok1 = d1[0] > PIVOT_FLOOR * m[3][0]
    l21 = df_div(e12, d1)
    l21 = tuple(jnp.where(ok1, v, 0.0) for v in l21)
    d2 = df_sub(d2, df_mul(l21, e12))
    y2 = df_sub(y2, df_mul(l21, y1))
    ok2 = ok1 & (d2[0] > PIVOT_FLOOR * m[5][0])
    c2 = tuple(jnp.where(ok2, v, 0.0) for v in df_div(y2, d2))
    c1 = tuple(jnp.where(ok1, v, 0.0) for v in df_div(y1, d1))
    c1 = df_sub(c1, df_mul(l21, c2))
    c0 = df_sub(df_sub(df_div(m[0], m[1]), df_mul(l10, c1)), df_mul(l20, c2))
    return c0[0], c1[0], c2[0]


def row_total(rows):
    s, e = two_sum(rows[0:8], rows[8:16])
    for step in (4, 2, 1):
        other = pltpu.roll(s, step, axis=0)
        e = e + pltpu.roll(e, step, axis=0)
        s, more = two_sum(s, other)
        e = e + more
    return s, e


def kernel(
    vel, coef, enth, void, cells, normal, flag,
    vel_out, p_out, h_out,
    field, tz, tlo, thi, cx, cy, czm, czp, av, wc, wn, wf, hot_row, hot_lane, grid,
    ho, po, vo, reduce, load_sem, store_sem, send_sem, recv_sem, sum_send, sum_recv,
):
    gx, gy, gz = lax.axis_index("gx"), lax.axis_index("gy"), lax.axis_index("gz")
    chip_y, core = gy // 2, lax.rem(gy, 2)
    has = (gx > 0, gx < NGX - 1, gy > 0, gy < NGY - 1, gz > 0, gz < NGZ - 1)
    beside = (
        (gx - 1, gy, gz), (gx + 1, gy, gz), (gx, gy - 1, gz),
        (gx, gy + 1, gz), (gx, gy, gz - 1), (gx, gy, gz + 1),
    )

    def in_plane(i, j):
        return (lax.rem(gx + i, NGX), lax.rem(chip_y + j, NGY // 2) * 2 + core, gz)

    def in_column(k, j):
        return (gx, chip_y * 2 + lax.rem(core + j, 2), lax.rem(gz + k, NGZ))

    plane = [in_plane(i, j) for i in range(NGX) for j in range(NGY // 2) if i or j]
    column = [in_column(k, j) for k in range(NGZ) for j in range(2) if k or j]
    across = (gx, lax.rem(gy + NGY - 1 + 2 * core, NGY), gz)

    barrier = pltpu.get_barrier_semaphore()
    partners = plane + column + [across]
    for partner in partners:
        pl.semaphore_signal(barrier, inc=1, device_id=partner, device_id_type=MESH)

    inner = (pl.ds(2, BX), pl.ds(8, BY))
    loads = [
        (cells, wc), (flag, wf), (normal, wn),
        (vel.at[0], field.at[(U0,) + inner]),
        (vel.at[pl.ds(1, 2)], field.at[(pl.ds(U1, 2),) + inner]),
        (coef, field.at[(C,) + inner]),
        (enth, field.at[(H,) + inner]),
        (void, av),
    ]
    loads = [pltpu.make_async_copy(s, d, load_sem.at[i]) for i, (s, d) in enumerate(loads)]
    for copy in loads:
        copy.start()

    blank = jnp.zeros((BY, BZ), jnp.float32)
    tile = jnp.zeros((8, BZ), jnp.float32)

    @pl.when(jnp.logical_not(has[0]))
    def _():
        for f in (U0, H, C, W0, W1, W2):
            field[f, 1, ROWS, :] = blank

    @pl.when(jnp.logical_not(has[1]))
    def _():
        for f in (U0, H, C, W0, W1, W2):
            field[f, 10, ROWS, :] = blank

    @pl.when(jnp.logical_not(has[2]))
    def _():
        for f in (H, C, U1, W0, W1, W2):
            for x in range(BX):
                field[f, x + 2, 7:8, :] = tile[0:1]

    @pl.when(jnp.logical_not(has[3]))
    def _():
        for f in (H, C, U1, W0, W1, W2):
            for x in range(BX):
                field[f, x + 2, 40:41, :] = tile[0:1]

    @pl.when(jnp.logical_not(has[4]))
    def _():
        for f in range(6):
            tlo[f] = tile

    @pl.when(jnp.logical_not(has[5]))
    def _():
        for f in range(6):
            thi[f] = tile

    lane8 = lax.broadcasted_iota(jnp.int32, (8, BZ), 1)
    lane32 = lax.broadcasted_iota(jnp.int32, (BY, BZ), 1)
    first, last = lane32 == 0, lane32 == BZ - 1

    def exchange(e, moves):
        copies = []
        for side, (src, dst) in enumerate(moves):
            copy = pltpu.make_async_remote_copy(
                src_ref=src, dst_ref=dst, send_sem=send_sem.at[e, side],
                recv_sem=recv_sem.at[e, side], device_id=beside[side], device_id_type=MESH,
            )
            pl.when(has[side])(copy.start)
            copies.append(copy)
        return copies

    def receive(copies):
        for side, copy in enumerate(copies):
            pl.when(has[side ^ 1])(copy.wait_recv)

    def moves_of(fx, fy, t):
        rows = pl.ds(8, BY)
        planes = pl.ds(2, BX)
        return (
            (field.at[fx, 2, rows], field.at[fx, 10, rows]),
            (field.at[fx, 9, rows], field.at[fx, 1, rows]),
            (field.at[fy, planes, 8], field.at[fy, planes, 40]),
            (field.at[fy, planes, 39], field.at[fy, planes, 7]),
            (tz.at[t], thi.at[t]),
            (tz.at[t], tlo.at[t]),
        )

    def pack(values, acc, x):
        for b in range(4):
            k = 4 * x + b
            turned = pltpu.roll(values[8 * b : 8 * b + 8], (4 * k + 2) % BZ, axis=1)
            acc = turned if acc is None else jnp.where(lane8 // 4 == k, turned, acc)
        return acc

    def joined(t):
        low = pltpu.roll(tlo[t], 1, axis=1)
        high = pltpu.roll(thi[t], BZ - 1, axis=1)
        return jnp.where(lane8 % 4 == 1, high, low)

    def around_z(values, halo, x):
        ends = jnp.concatenate(
            [pltpu.roll(halo, (2 * BZ - 4 * (4 * x + b) - 2) % BZ, axis=1) for b in range(4)], axis=0
        )
        after = jnp.where(last, ends, pltpu.roll(values, BZ - 1, axis=1))
        before = jnp.where(first, ends, pltpu.roll(values, 1, axis=1))
        return after, before

    def around_y(f, x):
        return field[f, x + 2, 9:41, :], field[f, x + 2, 7:39, :]

    def centre(f, x):
        return field[f, x + 2, ROWS, :]

    for copy in loads[0:3]:
        copy.wait()
    where = wc[...]
    row_of = where // BZ
    lane_of = where - row_of * BZ
    code = jnp.where(wf[...] > 0, wf[...] + 4 * (wn[...] // 2), 0).astype(jnp.float32)
    up256 = lax.broadcasted_iota(jnp.int32, (BX * BY, BZ), 0)
    up128 = lax.broadcasted_iota(jnp.int32, (BZ, BZ), 0)
    for s in range(SLOTS):
        hot_row[:, s * BZ : (s + 1) * BZ] = jnp.where(up256 == row_of[s : s + 1], 1.0, 0.0).astype(jnp.bfloat16)
        hot_lane[:, s * BZ : (s + 1) * BZ] = jnp.where(up128 == lane_of[s : s + 1], code[s : s + 1], 0.0).astype(jnp.bfloat16)

    for copy in loads[3:7]:
        copy.wait()
    t_u2 = t_h = t_c = None
    for x in range(BX):
        t_u2 = pack(centre(U2, x), t_u2, x)
        t_h = pack(centre(H, x), t_h, x)
        t_c = pack(centre(C, x), t_c, x)
    tz[TZ_U2] = t_u2
    tz[TZ_H] = t_h
    tz[TZ_C] = t_c
    pl.semaphore_wait(barrier, len(partners))
    ex0 = exchange(0, moves_of(pl.ds(U0, 3), pl.ds(H, 3), pl.ds(0, 3)))

    grid[...] = lax.dot_general(
        hot_row[...], hot_lane[...], (((1,), (1,)), ((), ())), preferred_element_type=jnp.float32
    )
    loads[7].wait()
    for x in range(BX):
        a = av[x]
        g = grid[x * BY : (x + 1) * BY, :]
        not_x = g > 3.5
        is_z = g > 7.5
        s = g - jnp.where(not_x, 4.0, 0.0) - jnp.where(is_z, 4.0, 0.0)
        u0, u1, u2 = centre(U0, x), centre(U1, x), centre(U2, x)
        parallel = (
            jnp.where(not_x, u0 * u0, 0.0)
            + jnp.where(not_x & jnp.logical_not(is_z), 0.0, u1 * u1)
            + jnp.where(is_z, 0.0, u2 * u2)
        )
        speed = jnp.sqrt(parallel + 0.25)
        liquid = 1.0 - a
        evap = 1.5 * a * s * s
        root = jnp.where(s > 1.5, 2.0 * 1.4142135623730951, s)
        heat = liquid * speed * s + 0.6 * liquid * root + evap
        vo[0, x] = heat
        vo[1, x] = evap

    receive(ex0)
    zu, zh, zc = joined(TZ_U2), joined(TZ_H), joined(TZ_C)
    tb = None
    for x in range(BX):
        u2p, u2m = around_z(centre(U2, x), zu, x)
        u1p, u1m = around_y(U1, x)
        u0p, u0m = field[U0, x + 3, ROWS, :], field[U0, x + 1, ROWS, :]
        diverge = 0.5 * (u0p - u0m + (u1p - u1m) + (u2p - u2m))
        b = EXPANSION * (0.5 * vo[1, x]) - diverge
        field[W0, x + 2, ROWS, :] = b
        tb = pack(b, tb, x)
    tz[TZ_W0] = tb
    ex1 = exchange(1, moves_of(W0, W0, TZ_W0))

    half = 0.5 / SCALE
    for x in range(BX):
        c = centre(C, x)
        if x == 0:
            cx[0] = half * (c + field[C, 1, ROWS, :])
        cx[x + 1] = half * (c + field[C, x + 3, ROWS, :])
        after, before = around_y(C, x)
        cy[x, 0:32] = half * (c + before)
        cy[x, 32:33] = half * (c[31:32] + after[31:32])
        after, before = around_z(c, zc, x)
        czp[x] = half * (c + after)
        czm[x] = half * (c + before)
        h = centre(H, x)
        hyp, hym = around_y(H, x)
        hzp, hzm = around_z(h, zh, x)
        laplace = field[H, x + 3, ROWS, :] + field[H, x + 1, ROWS, :] + hyp + hym + hzp + hzm - 6.0 * h
        ho[x] = h + DIFFUSE * laplace + HEATING * vo[0, x]
    store_h = pltpu.make_async_copy(ho, h_out, store_sem.at[0])
    store_h.start()

    def fold(v):
        return (v[0:8] + v[8:16]) + (v[16:24] + v[24:32])

    def plus(acc, v):
        v = fold(v)
        return v if acc is None else acc + v

    def operator(f, t, x, halo):
        v = centre(f, x)
        yp, ym = around_y(f, x)
        zp, zm = around_z(v, halo, x)
        out = cx[x + 1] * (v - field[f, x + 3, ROWS, :]) + cx[x] * (v - field[f, x + 1, ROWS, :])
        out = out + (cy[x, 1:33] * (v - yp) + cy[x, 0:32] * (v - ym))
        out = out + (czp[x] * (v - zp) + czm[x] * (v - zm))
        return v, out

    m = [None] * 6
    receive(ex1)
    z0 = joined(TZ_W0)
    tb = None
    for x in range(BX):
        v, out = operator(W0, TZ_W0, x, z0)
        field[W1, x + 2, ROWS, :] = out
        tb = pack(out, tb, x)
    tz[TZ_W1] = tb
    ex2 = exchange(2, moves_of(W1, W1, TZ_W1))
    for x in range(BX):
        v, out = centre(W0, x), centre(W1, x)
        m[0], m[1], m[2] = plus(m[0], v * v), plus(m[1], v * out), plus(m[2], out * out)
    receive(ex2)
    z1 = joined(TZ_W1)
    tb = None
    for x in range(BX):
        v, out = operator(W1, TZ_W1, x, z1)
        field[W2, x + 2, ROWS, :] = out
        tb = pack(out, tb, x)
    tz[TZ_W2] = tb
    ex3 = exchange(3, moves_of(W2, W2, TZ_W2))
    for x in range(BX):
        v, out = centre(W1, x), centre(W2, x)
        m[3], m[4] = plus(m[3], v * out), plus(m[4], out * out)
    receive(ex3)
    z2 = joined(TZ_W2)
    for x in range(BX):
        v, out = operator(W2, TZ_W2, x, z2)
        m[5] = plus(m[5], v * out)

    row = jnp.zeros((1, BZ), jnp.float32)
    for i in range(6):
        row = jnp.where(lane8[0:1] == i, jnp.sum(m[i], keepdims=True), row)

    def all_sum(phase, row, group):
        reduce[phase, 0:1, :] = row
        copies = []
        for slot, partner in enumerate(group):
            copy = pltpu.make_async_remote_copy(
                src_ref=reduce.at[phase, pl.ds(0, 1)], dst_ref=reduce.at[phase, pl.ds(slot + 1, 1)],
                send_sem=sum_send.at[phase, slot], recv_sem=sum_recv.at[phase, slot],
                device_id=partner, device_id_type=MESH,
            )
            copy.start()
            copies.append(copy)
        for copy in copies:
            copy.wait_recv()
        return copies, row_total(reduce[phase])

    sums0, (high, low) = all_sum(0, row, plane)
    row = jnp.where(lane8 < 8, high, pltpu.roll(low, 8, axis=1))[0:1]
    sums1, (high, low) = all_sum(1, row, column)
    for copies in (ex0, ex1, ex2, ex3):
        for side, copy in enumerate(copies):
            pl.when(has[side])(copy.wait_send)
    low = low + pltpu.roll(high, BZ - 8, axis=1)
    moments = [quick_sum(high[0:1, i : i + 1], low[0:1, i : i + 1]) for i in range(6)]
    c0, c1, c2 = (v * (1.0 / SCALE) for v in solve_moments(moments))

    def mix(a, b, c):
        return c0 * a + c1 * b + c2 * c

    def pressure(planes, rows):
        return mix(field[W0, planes, rows, :], field[W1, planes, rows, :], field[W2, planes, rows, :])

    for x in range(-1, BX + 1):
        field[H, x + 2, ROWS, :] = pressure(x + 2, ROWS)
    for x in range(BX):
        for y in (7, 40):
            field[H, x + 2, y : y + 1, :] = pressure(x + 2, slice(y, y + 1))
        po[x] = centre(H, x)
    store_p = pltpu.make_async_copy(po, p_out, store_sem.at[1])
    store_p.start()
    zp = mix(z0, z1, z2)
    for x in range(BX):
        c = 0.5 * centre(C, x)
        after, before = around_y(H, x)
        vo[1, x] = centre(U1, x) - c * (after - before)
        after, before = around_z(centre(H, x), zp, x)
        vo[2, x] = centre(U2, x) - c * (after - before)
        vo[0, x] = centre(U0, x) - c * (field[H, x + 3, ROWS, :] - field[H, x + 1, ROWS, :])
    store_v = pltpu.make_async_copy(vo, vel_out, store_sem.at[2])
    store_v.start()
    for copy in sums0 + sums1:
        copy.wait_send()
    store_h.wait()
    store_p.wait()
    store_v.wait()


def shards(*args):
    block = (BX, BY, BZ)
    f32 = jnp.float32
    any_ref = pl.BlockSpec(memory_space=pl.ANY)
    return tuple(
        pl.pallas_call(
            kernel,
            out_shape=(
                jax.ShapeDtypeStruct((3,) + block, f32),
                jax.ShapeDtypeStruct(block, f32),
                jax.ShapeDtypeStruct(block, f32),
            ),
            in_specs=[any_ref] * 7,
            out_specs=(any_ref,) * 3,
            scratch_shapes=[
                pltpu.VMEM((8, BX + 4, BY + 16, BZ), f32),
                pltpu.VMEM((6, 8, BZ), f32),
                pltpu.VMEM((6, 8, BZ), f32),
                pltpu.VMEM((6, 8, BZ), f32),
                pltpu.VMEM((BX + 1, BY, BZ), f32),
                pltpu.VMEM((BX, BY + 8, BZ), f32),
                pltpu.VMEM(block, f32),
                pltpu.VMEM(block, f32),
                pltpu.VMEM(block, f32),
                pltpu.VMEM((SLOTS, BZ), jnp.int32),
                pltpu.VMEM((SLOTS, BZ), jnp.int32),
                pltpu.VMEM((SLOTS, BZ), jnp.int32),
                pltpu.VMEM((BX * BY, SLOTS * BZ), jnp.bfloat16),
                pltpu.VMEM((BZ, SLOTS * BZ), jnp.bfloat16),
                pltpu.VMEM((BX * BY, BZ), f32),
                pltpu.VMEM(block, f32),
                pltpu.VMEM(block, f32),
                pltpu.VMEM((3,) + block, f32),
                pltpu.VMEM((2, 16, BZ), f32),
                pltpu.SemaphoreType.DMA((8,)),
                pltpu.SemaphoreType.DMA((3,)),
                pltpu.SemaphoreType.DMA((4, 6)),
                pltpu.SemaphoreType.DMA((4, 6)),
                pltpu.SemaphoreType.DMA((2, 15)),
                pltpu.SemaphoreType.DMA((2, 15)),
            ],
            compiler_params=pltpu.CompilerParams(
                collective_id=0, has_side_effects=True, vmem_limit_bytes=24 * 1024 * 1024
            ),
            name="simple_step",
        )(*args)
    )


def solution(mesh):
    in_specs = (
        P(None, "gx", "gy", "gz"),
        P("gx", "gy", "gz"),
        P("gx", "gy", "gz"),
        P("gx", "gy", "gz"),
        P(("gx", "gy", "gz"), None),
        P(("gx", "gy", "gz"), None),
        P(("gx", "gy", "gz"), None),
    )
    out_specs = (P(None, "gx", "gy", "gz"), P("gx", "gy", "gz"), P("gx", "gy", "gz"))
    return jax.shard_map(shards, mesh=mesh, in_specs=in_specs, out_specs=out_specs, check_vma=False)
```

time: 603 us -> 46 us (0.08)
  blocking collectives: 382 us -> 0 us
  starting transfers between devices: 76.3 us -> 0 us
  other arithmetic: 50.1 us -> 0 us
  waiting for transfers between devices: 40.4 us -> 0 us
  Pallas kernels: 0 us -> 37.2 us
  local copies, waits for them, and re-layouts: 43.9 us -> 7.85 us
  between operations: 8.01 us -> 0.66 us
    psum x5 -> x0, blocking collectives: 382 us -> none  [the longest x3 229 us: squares(): return lax.psum(jnp.sum(field * field), ('gx', 'gy', 'gz'))]
    ppermute x30 -> x0, starting transfers between devices: 76.3 us -> none  [the longest x15 53.6 us: with_halo(): before = lax.ppermute(last, axis, up)]
    ppermute x30 -> x0, waiting for transfers between devices: 40.4 us -> none  [the longest x15 33.4 us: with_halo(): after = lax.ppermute(first, axis, down)]
    pallas_call x0 -> x1, Pallas kernels: none -> 37.2 us  [shards(): pl.pallas_call(kernel, out_shape=(jax.ShapeDtypeStruct((3,) + block, f32)...]
    gather x2 -> x0, local copies, waits for them, and re-layouts: 23 us -> none  [the longest x1 11.8 us: shards(): void_cells = void.reshape(cells)[wall_cells]]
    mul x3 -> x0, other arithmetic: 22.5 us -> none  [the longest x1 22.2 us: balance_terms(): enthalpy_new = centre_h + DIFFUSE * laplace + HEATING * heat_source]
    scatter-add x1 -> x0, other arithmetic: 18.2 us -> none  [shards(): sources.at[:, wall_cells.reshape(-1)]]
    mul x1 -> x0, local copies, waits for them, and re-layouts: 8.23 us -> none  [balance_terms(): 0.5 * (near_u[0][0] - near_u[1][0] + (near_u[2][1] - near_u[3][1]) + (nea...]
  transfers between devices with their start and end apart: 30 -> 0, of which waited for: 17 -> 0; matrix products, arithmetic and copies ran while one was open for 9% -> 0% of each run, Pallas kernels for 0% -> 0%
where the time goes in v1:
time: 46 us; the launch traced here: 45.7 us
  Pallas kernels  37.2 us (81%)
  local copies, waits for them, and re-layouts  7.85 us (17%)
  between operations  0.66 us (1%)
    pallas_call x1, Pallas kernels, shards(): pl.pallas_call(kernel, out_shape=(jax.ShapeDtypeStruct((3,) + block, f32)...  37.2 us
    unnamed x17, local copies, waits for them, and re-layouts  7.85 us

profile of v1, /device:TPU:1, one launch (start us, length us, event | category | flops | bytes accessed | tf_op | source)
XLA Modules:
  0.0 45.7 jit_solution(12236358875314130818)
XLA Ops:
  0.6 0.0 copy-start
  0.6 1.0 %copy-done = f32[3,8,32,128]{3,2,1,0:T(8,128)S(1)} copy-done((f32[3,8,32,128]{3,2,1,0:T(8,128)S(1)}, f32[3,8,32,128]{3,2,1,0:T(8,128)}, u32[]{:S(2)}) %copy-start) | copy-done | bytes 393240
  1.6 0.0 copy-start.1
  1.6 0.9 %copy-done.1 = f32[8,32,128]{2,1,0:T(8,128)S(1)} copy-done((f32[8,32,128]{2,1,0:T(8,128)S(1)}, f32[8,32,128]{2,1,0:T(8,128)}, u32[]{:S(2)}) %copy-start.1) | copy-done | bytes 131096
  2.5 0.0 copy-start.2
  2.5 0.9 %copy-done.2 = f32[8,32,128]{2,1,0:T(8,128)S(1)} copy-done((f32[8,32,128]{2,1,0:T(8,128)S(1)}, f32[8,32,128]{2,1,0:T(8,128)}, u32[]{:S(2)}) %copy-start.2) | copy-done | bytes 131096
  3.4 0.0 copy-start.3
  3.4 0.9 %copy-done.3 = f32[8,32,128]{2,1,0:T(8,128)S(1)} copy-done((f32[8,32,128]{2,1,0:T(8,128)S(1)}, f32[8,32,128]{2,1,0:T(8,128)}, u32[]{:S(2)}) %copy-start.3) | copy-done | bytes 131096
  4.3 0.0 copy-start.4
  4.3 0.7 %copy-done.4 = s32[16,128]{1,0:T(8,128)S(1)} copy-done((s32[16,128]{1,0:T(8,128)S(1)}, s32[16,128]{1,0:T(8,128)}, u32[]{:S(2)}) %copy-start.4) | copy-done | bytes 8216
  5.0 0.0 copy-start.5
  5.0 0.7 %copy-done.5 = s32[16,128]{1,0:T(8,128)S(1)} copy-done((s32[16,128]{1,0:T(8,128)S(1)}, s32[16,128]{1,0:T(8,128)}, u32[]{:S(2)}) %copy-start.5) | copy-done | bytes 8216
  5.7 0.0 copy-start.6
  5.7 0.7 %copy-done.6 = s32[16,128]{1,0:T(8,128)S(1)} copy-done((s32[16,128]{1,0:T(8,128)S(1)}, s32[16,128]{1,0:T(8,128)}, u32[]{:S(2)}) %copy-start.6) | copy-done | bytes 8216
  6.4 37.2 %simple_step.1 = (f32[3,8,32,128]{3,2,1,0:T(8,128)S(1)}, f32[8,32,128]{2,1,0:T(8,128)S(1)}, f32[8,32,128]{2,1,0:T(8,128)S(1)}) custom-call(f32[3,8,32,128]{3,2,1,0:T(8,128)S(1)} %copy-done, f32[8,32,128]{2,1,0:T(8,128)S(1)} %copy-done.1, f32[8,32,128]{2,1,0:T(8,128)S(1)} %copy-done.2, f32[8,32,128]{2,1,0:T(8,128)S(1)} %copy-done.3, s32[16,128]{1,0:T(8,128)S(1)} %copy-done.4, ...), custom_call_target="tpu_custom_call" | custom-call | tf_op jit(solution)/shard_map/simple_step/pallas_call | solution.py:423
  43.6 0.7 %copy.13 = f32[3,8,32,128]{3,2,1,0:T(8,128)} copy(f32[3,8,32,128]{3,2,1,0:T(8,128)S(1)} %get-tuple-element.6) | data formatting | bytes 786432
  44.4 0.7 %copy.14 = f32[8,32,128]{2,1,0:T(8,128)} copy(f32[8,32,128]{2,1,0:T(8,128)S(1)} %get-tuple-element.7) | data formatting | bytes 262144
  45.0 0.7 %copy.15 = f32[8,32,128]{2,1,0:T(8,128)} copy(f32[8,32,128]{2,1,0:T(8,128)S(1)} %get-tuple-element.8) | data formatting | bytes 262144
Async XLA Ops:
  0.6 1.0 %copy-start = (f32[3,8,32,128]{3,2,1,0:T(8,128)S(1)}, f32[3,8,32,128]{3,2,1,0:T(8,128)}, u32[]{:S(2)}) copy-start(f32[3,8,32,128]{3,2,1,0:T(8,128)} %vel.1) | copy-start | bytes 1179652
  1.6 0.9 %copy-start.1 = (f32[8,32,128]{2,1,0:T(8,128)S(1)}, f32[8,32,128]{2,1,0:T(8,128)}, u32[]{:S(2)}) copy-start(f32[8,32,128]{2,1,0:T(8,128)} %coef.1) | copy-start | bytes 393220
  2.5 0.9 %copy-start.2 = (f32[8,32,128]{2,1,0:T(8,128)S(1)}, f32[8,32,128]{2,1,0:T(8,128)}, u32[]{:S(2)}) copy-start(f32[8,32,128]{2,1,0:T(8,128)} %enth.1) | copy-start | bytes 393220
  3.4 0.9 %copy-start.3 = (f32[8,32,128]{2,1,0:T(8,128)S(1)}, f32[8,32,128]{2,1,0:T(8,128)}, u32[]{:S(2)}) copy-start(f32[8,32,128]{2,1,0:T(8,128)} %void.1) | copy-start | bytes 393220
  4.3 0.7 %copy-start.4 = (s32[16,128]{1,0:T(8,128)S(1)}, s32[16,128]{1,0:T(8,128)}, u32[]{:S(2)}) copy-start(s32[16,128]{1,0:T(8,128)} %cells.1) | copy-start | bytes 24580
  5.0 0.7 %copy-start.5 = (s32[16,128]{1,0:T(8,128)S(1)}, s32[16,128]{1,0:T(8,128)}, u32[]{:S(2)}) copy-start(s32[16,128]{1,0:T(8,128)} %normal.1) | copy-start | bytes 24580
  5.7 0.7 %copy-start.6 = (s32[16,128]{1,0:T(8,128)S(1)}, s32[16,128]{1,0:T(8,128)}, u32[]{:S(2)}) copy-start(s32[16,128]{1,0:T(8,128)} %flag.1) | copy-start | bytes 24580

commit v2 on v1

v2 whole, which is shorter than its diff:
```python
import jax
import jax.numpy as jnp
from jax import lax
from jax.experimental import pallas as pl
from jax.experimental.pallas import tpu as pltpu
from jax.sharding import PartitionSpec as P

MESH = pl.DeviceIdType.MESH
NGX, NGY, NGZ = 4, 8, 8
BX, BY, BZ = 8, 32, 128
SLOTS = 16
DIFFUSE = 0.1
HEATING = 0.5
EXPANSION = 1.5
SCALE = 16.0
H, C, U0, U1, U2, BP, W0, W1, W2 = range(9)
FIELDS = 9
TU0, TC, TU2, TU1, TH, TB, TW = range(7)
ROWS = slice(8, 40)
SIGNS = (-1, 1)
XZ = tuple((a, 0, c) for a in SIGNS for c in SIGNS)
YZ = tuple((0, b, c) for b in SIGNS for c in SIGNS)
XY = tuple((a, b, 0) for a in SIGNS for b in SIGNS)
SIDES = ((-1, 0, 0), (1, 0, 0), (0, -1, 0), (0, 1, 0), (0, 0, -1), (0, 0, 1)) + XY + XZ + YZ
EARLY, LATE, ENTH, IMAGE = range(4)
PIVOT_FLOOR = 1e-9


def two_sum(a, b):
    s = a + b
    t = s - a
    return s, (a - (s - t)) + (b - t)


def quick_sum(a, b):
    s = a + b
    return s, b - (s - a)


def split(a):
    t = 4097.0 * a
    high = t - (t - a)
    return high, a - high


def two_mul(a, b):
    p = a * b
    ah, al = split(a)
    bh, bl = split(b)
    return p, ((ah * bh - p) + ah * bl + al * bh) + al * bl


def df_sub(a, b):
    s, e = two_sum(a[0], -b[0])
    return quick_sum(s, e + (a[1] - b[1]))


def df_mul(a, b):
    p, e = two_mul(a[0], b[0])
    return quick_sum(p, e + (a[0] * b[1] + a[1] * b[0]))


def df_div(a, b):
    q = a[0] / b[0]
    p, e = two_mul(q, b[0])
    rest = ((a[0] - p) - e) + a[1] - q * b[1]
    return quick_sum(q, rest / b[0])


def solve_moments(m):
    l10 = df_div(m[2], m[1])
    l20 = df_div(m[3], m[1])
    d1 = df_sub(m[3], df_mul(l10, m[2]))
    e12 = df_sub(m[4], df_mul(l10, m[3]))
    y1 = df_sub(m[1], df_mul(l10, m[0]))
    y2 = df_sub(m[2], df_mul(l20, m[0]))
    d2 = df_sub(m[5], df_mul(l20, m[3]))
    ok1 = d1[0] > PIVOT_FLOOR * m[3][0]
    l21 = df_div(e12, d1)
    l21 = tuple(jnp.where(ok1, v, 0.0) for v in l21)
    d2 = df_sub(d2, df_mul(l21, e12))
    y2 = df_sub(y2, df_mul(l21, y1))
    ok2 = ok1 & (d2[0] > PIVOT_FLOOR * m[5][0])
    c2 = tuple(jnp.where(ok2, v, 0.0) for v in df_div(y2, d2))
    c1 = tuple(jnp.where(ok1, v, 0.0) for v in df_div(y1, d1))
    c1 = df_sub(c1, df_mul(l21, c2))
    c0 = df_sub(df_sub(df_div(m[0], m[1]), df_mul(l10, c1)), df_mul(l20, c2))
    return c0[0], c1[0], c2[0]


def row_total(rows):
    s, e = two_sum(rows[0:8], rows[8:16])
    for step in (4, 2, 1):
        other = pltpu.roll(s, step, axis=0)
        e = e + pltpu.roll(e, step, axis=0)
        s, more = two_sum(s, other)
        e = e + more
    return s, e


def opposite(side):
    return tuple(-v for v in side)


def messages(field, tz, tlo, thi, dz):
    xs, xd = {-1: 2, 1: 9}, {-1: 10, 1: 1}
    ys, yd = {-1: 8, 1: 39}, {-1: 40, 1: 7}
    xs2, xd2 = {-1: pl.ds(2, 2), 1: pl.ds(8, 2)}, {-1: pl.ds(10, 2), 1: pl.ds(0, 2)}
    ys2, yd2 = {-1: pl.ds(8, 2), 1: pl.ds(38, 2)}, {-1: pl.ds(40, 2), 1: pl.ds(6, 2)}
    rows, planes = pl.ds(8, BY), pl.ds(2, BX)
    table = [{}, {}, {}, {}]
    for side in SIDES:
        a, b, c = side
        far = thi if c < 0 else tlo
        slot = (XZ + YZ).index(opposite(side)) if side in XZ + YZ else None
        if side in XZ:
            early = [(tz.at[pl.ds(TU0, 3)], dz.at[slot, pl.ds(0, 3)])]
            image = [(tz.at[TW], dz.at[slot, 3])]
            late = enth = []
        elif side in YZ:
            early = [(tz.at[pl.ds(TC, 3)], dz.at[slot, pl.ds(0, 3)])]
            image = [(tz.at[TW], dz.at[slot, 3])]
            late = enth = []
        elif side in XY:
            early = [(field.at[pl.ds(C, 3), xs[a], ys[b]], field.at[pl.ds(C, 3), xd[a], yd[b]])]
            image = [(field.at[W1, xs[a], ys[b]], field.at[W1, xd[a], yd[b]])]
            late = enth = []
        elif a:
            early = [
                (field.at[C, xs2[a], rows], field.at[C, xd2[a], rows]),
                (field.at[U0, xs[a], rows], field.at[U0, xd[a], rows]),
            ]
            late = [(field.at[BP, xs[a], rows], field.at[BP, xd[a], rows])]
            enth = [(field.at[H, xs[a], rows], field.at[H, xd[a], rows])]
            image = [(field.at[W1, xs2[a], rows], field.at[W1, xd2[a], rows])]
        elif b:
            early = [
                (field.at[C, planes, ys2[b]], field.at[C, planes, yd2[b]]),
                (field.at[U1, planes, ys[b]], field.at[U1, planes, yd[b]]),
            ]
            late = [(field.at[BP, planes, ys[b]], field.at[BP, planes, yd[b]])]
            enth = [(field.at[H, planes, ys[b]], field.at[H, planes, yd[b]])]
            image = [(field.at[W1, planes, ys2[b]], field.at[W1, planes, yd2[b]])]
        else:
            early = [(tz.at[pl.ds(TC, 2)], far.at[pl.ds(TC, 2)])]
            late = [(tz.at[TB], far.at[TB])]
            enth = [(tz.at[TH], far.at[TH])]
            image = [(tz.at[TW], far.at[TW])]
        for kind, pairs in ((EARLY, early), (LATE, late), (ENTH, enth), (IMAGE, image)):
            table[kind][side] = pairs
    return table


N_MESSAGES = 22 + 6 + 6 + 18


def kernel(
    vel, coef, enth, void, cells, normal, flag,
    w_out, g_out, u_out, h_out, c_out,
    field, tz, tlo, thi, dz, cx, cy, czm, czp, zlow, av, wc, wn, wf, hot_row, hot_lane, grid,
    heat, reduce, load_sem, copy_sem, send_sem, recv_sem, sum_send, sum_recv,
):
    gx, gy, gz = lax.axis_index("gx"), lax.axis_index("gy"), lax.axis_index("gz")
    chip_y, core = gy // 2, lax.rem(gy, 2)

    def exists(side):
        found = None
        for at, step, size in zip((gx, gy, gz), side, (NGX, NGY, NGZ)):
            if step:
                inside = at > 0 if step < 0 else at < size - 1
                found = inside if found is None else found & inside
        return found

    has = {side: exists(side) for side in SIDES}

    def in_plane(i, j):
        return (lax.rem(gx + i, NGX), lax.rem(chip_y + j, NGY // 2) * 2 + core, gz)

    def in_column(k, j):
        return (gx, chip_y * 2 + lax.rem(core + j, 2), lax.rem(gz + k, NGZ))

    def far_first(pairs, n, m):
        return sorted(pairs, key=lambda p: -min(p[0], n - p[0]) - min(p[1], m - p[1]))

    plane = [in_plane(i, j) for i, j in far_first([(i, j) for i in range(NGX) for j in range(NGY // 2) if i or j], NGX, NGY // 2)]
    column = [in_column(k, j) for k, j in far_first([(k, j) for k in range(NGZ) for j in range(2) if k or j], NGZ, 2)]

    inner = (pl.ds(2, BX), pl.ds(8, BY))
    loads = [
        (cells, wc), (flag, wf), (normal, wn),
        (vel, field.at[(pl.ds(U0, 3),) + inner]),
        (void, av),
        (coef, field.at[(C,) + inner]),
        (enth, field.at[(H,) + inner]),
    ]
    loads = [pltpu.make_async_copy(s, d, load_sem.at[i]) for i, (s, d) in enumerate(loads)]
    for copy in loads:
        copy.start()

    barrier = pltpu.get_barrier_semaphore()
    for partner in column + plane:
        pl.semaphore_signal(barrier, inc=1, device_id=partner, device_id_type=MESH)
    expected = len(plane) + len(column)
    for side in SIDES:
        a, b, c = side
        if (a and not b and not c) or (c and not a and not b):
            continue
        met = has[side]
        if b and not a:
            met = met & (core == (0 if b < 0 else 1))

        @pl.when(met)
        def _():
            pl.semaphore_signal(barrier, inc=1, device_id=(gx + a, gy + b, gz + c), device_id_type=MESH)

        expected = expected + met.astype(jnp.int32)

    table = messages(field, tz, tlo, thi, dz)
    copies = [{}, {}, {}, {}]
    at = 0
    for kind in range(4):
        for side in SIDES:
            copies[kind][side] = []
            for src, dst in table[kind][side]:
                copies[kind][side].append(
                    pltpu.make_async_remote_copy(
                        src_ref=src, dst_ref=dst, send_sem=send_sem.at[at], recv_sem=recv_sem.at[at],
                        device_id=(gx + side[0], gy + side[1], gz + side[2]), device_id_type=MESH,
                    )
                )
                at += 1

    def send(kind, sides):
        for side in sides:
            if copies[kind][side]:

                @pl.when(has[side])
                def _():
                    for copy in copies[kind][side]:
                        copy.start()

    def receive(kind):
        for side in SIDES:
            if copies[kind][side]:

                @pl.when(has[opposite(side)])
                def _():
                    for copy in copies[kind][side]:
                        copy.wait_recv()

    for side in SIDES:

        @pl.when(jnp.logical_not(has[opposite(side)]))
        def _():
            for kind in range(4):
                for _, dst in table[kind][side]:
                    dst[...] = jnp.zeros(dst.shape, jnp.float32)

    lane8 = lax.broadcasted_iota(jnp.int32, (8, BZ), 1)
    sub8 = lax.broadcasted_iota(jnp.int32, (8, BZ), 0)
    lane32 = lax.broadcasted_iota(jnp.int32, (BY, BZ), 1)
    row32 = lax.broadcasted_iota(jnp.int32, (BY, BZ), 0)
    first, last = lane32 == 0, lane32 == BZ - 1
    first8, last8 = lane8 == 0, lane8 == BZ - 1
    place = lane8 % 4
    low_lane = place == 1
    y_group = lane8 // 4 % 4
    ends_half = jnp.where(first8, 0.5, jnp.where(last8, -0.5, 0.0))
    ends_half32 = jnp.where(first, 0.5, jnp.where(last, -0.5, 0.0))

    def turn(v, by, axis=1):
        size = v.shape[axis]
        return pltpu.roll(v, by % size, axis=axis) if by % size else v

    def pack(values, acc, x):
        for b in range(4):
            k = 4 * x + b
            turned = turn(values[8 * b : 8 * b + 8], 4 * k + 2)
            acc = turned if acc is None else jnp.where(lane8 // 4 == k, turned, acc)
        return acc

    def pair(low, high):
        return jnp.where(low_lane, low, high)

    def swap(v):
        return jnp.where(low_lane, turn(v, -1), turn(v, 1))

    def ends(swapped, x):
        return jnp.concatenate([turn(swapped, -4 * (4 * x + b) - 2) for b in range(4)], axis=0)

    def ends_row(swapped, b):
        row, k = (7, 3) if b < 0 else (0, 0)
        out = None
        spread = jnp.broadcast_to(swapped[row : row + 1], (8, BZ))
        for x in range(BX):
            turned = turn(spread, -4 * (4 * x + k) - 2)
            out = turned if out is None else jnp.where(sub8 == x, turned, out)
        return out

    def around_z(v, e):
        f, l = (first, last) if v.shape[0] == BY else (first8, last8)
        return jnp.where(l, e, turn(v, -1)), jnp.where(f, e, turn(v, 1))

    def around_y(f, x):
        return field[f, x + 2, 9:41, :], field[f, x + 2, 7:39, :]

    def centre(f, x):
        return field[f, x + 2, ROWS, :]

    def row_of_field(f, r):
        return field[f, 2:10, r, :]

    def diagonal(side, q):
        a, b, _ = side
        lo, hi = ((XZ + YZ).index((a, b, c)) for c in SIGNS)
        return pair(dz[lo, q], dz[hi, q])

    xm_side, xp_side, ym_side, yp_side, zm_side, zp_side = SIDES[:6]

    for copy in loads[0:3]:
        copy.wait()
    where = wc[...]
    row_at = where // BZ
    lane_at = where - row_at * BZ
    code = jnp.where(wf[...] > 0, wf[...] + 4 * (wn[...] // 2), 0).astype(jnp.float32)
    up256 = lax.broadcasted_iota(jnp.int32, (BX * BY, BZ), 0)
    up128 = lax.broadcasted_iota(jnp.int32, (BZ, BZ), 0)
    for s in range(SLOTS):
        hot_row[:, s * BZ : (s + 1) * BZ] = jnp.where(up256 == row_at[s : s + 1], 1.0, 0.0).astype(jnp.bfloat16)
        hot_lane[:, s * BZ : (s + 1) * BZ] = jnp.where(up128 == lane_at[s : s + 1], code[s : s + 1], 0.0).astype(jnp.bfloat16)
    grid[...] = lax.dot_general(
        hot_row[...], hot_lane[...], (((1,), (1,)), ((), ())), preferred_element_type=jnp.float32
    )
    for copy in loads[3:]:
        copy.wait()

    t_b = t_c = t_u0 = t_u1 = t_u2 = None
    for x in range(BX):
        a = av[x]
        g = grid[x * BY : (x + 1) * BY, :]
        not_x = g > 3.5
        is_z = g > 7.5
        s = g - jnp.where(not_x, 4.0, 0.0) - jnp.where(is_z, 4.0, 0.0)
        u0, u1, u2 = centre(U0, x), centre(U1, x), centre(U2, x)
        parallel = (
            jnp.where(not_x, u0 * u0, 0.0)
            + jnp.where(not_x & jnp.logical_not(is_z), 0.0, u1 * u1)
            + jnp.where(is_z, 0.0, u2 * u2)
        )
        speed = jnp.sqrt(parallel + 0.25)
        liquid = 1.0 - a
        evap = 1.5 * a * s * s
        root = jnp.where(s > 1.5, 2.0 * 1.4142135623730951, s)
        heat[x] = liquid * speed * s + 0.6 * liquid * root + evap
        slope = jnp.where(row32 == BY - 1, 0.0, turn(u1, -1, 0)) - jnp.where(row32 == 0, 0.0, turn(u1, 1, 0))
        slope = slope + (jnp.where(last, 0.0, turn(u2, -1)) - jnp.where(first, 0.0, turn(u2, 1)))
        if x < BX - 1:
            slope = slope + centre(U0, x + 1)
        if x > 0:
            slope = slope - centre(U0, x - 1)
        b = EXPANSION * (0.5 * evap) - 0.5 * slope
        field[BP, x + 2, ROWS, :] = b
        t_b = pack(b, t_b, x)
        t_c = pack(centre(C, x), t_c, x)
        t_u0 = pack(u0, t_u0, x)
        t_u1 = pack(u1, t_u1, x)
        t_u2 = pack(u2, t_u2, x)
    for i, t in ((TB, t_b), (TC, t_c), (TU0, t_u0), (TU1, t_u1), (TU2, t_u2)):
        tz[i] = t

    pl.semaphore_wait(barrier, expected)
    send(EARLY, XZ + YZ + XY)
    send(EARLY, SIDES[:6])
    send(LATE, SIDES[:6])

    t_h = None
    half = 0.5 / SCALE
    for x in range(BX):
        t_h = pack(centre(H, x), t_h, x)
        c = centre(C, x)
        if x < BX - 1:
            cx[x + 2] = half * (c + centre(C, x + 1))
        cy[x + 1, 0:32] = half * (c + turn(c, 1, 0))
        czp[x + 1] = half * jnp.where(last, c, c + turn(c, -1))
        czm[x + 1] = half * jnp.where(first, c, c + turn(c, 1))
    tz[TH] = t_h
    send(ENTH, SIDES[:6])

    def low_high(v):
        return v[0:8], v[8:24], v[24:32]

    def y_ends(v, f, x):
        a, m, z = low_high(v)
        a = a + jnp.where(sub8 == 0, 0.5 * field[f, x + 2, 7:8, :], 0.0)
        z = z - jnp.where(sub8 == 7, 0.5 * field[f, x + 2, 40:41, :], 0.0)
        return jnp.concatenate([a, m, z], axis=0)

    receive(EARLY)
    receive(LATE)
    s_u2 = swap(pair(tlo[TU2], thi[TU2]))
    s_c = swap(pair(tlo[TC], thi[TC]))
    for x in range(BX):
        b = centre(BP, x) + ends_half32 * ends(s_u2, x)
        b = y_ends(b, U1, x)
        if x == 0:
            b = b + 0.5 * field[U0, 1, ROWS, :]
        if x == BX - 1:
            b = b - 0.5 * field[U0, 10, ROWS, :]
        field[W0, x + 2, ROWS, :] = b
        c = centre(C, x)
        e = ends(s_c, x)
        czp[x + 1] = czp[x + 1] + jnp.where(last, half * e, 0.0)
        czm[x + 1] = czm[x + 1] + jnp.where(first, half * e, 0.0)
        cy[x + 1, 0:1] = half * (c[0:1] + field[C, x + 2, 7:8, :])
        cy[x + 1, 32:33] = half * (c[31:32] + field[C, x + 2, 40:41, :])
    cx[1] = half * (centre(C, 0) + centre(C, -1))
    cx[9] = half * (centre(C, 7) + centre(C, 8))
    for x, own, sign, side, inside in ((-1, 0, -0.5, xm_side, 7), (BX, BX - 1, 0.5, xp_side, 0)):
        b = centre(BP, x) + sign * centre(U0, own)
        b = y_ends(b, U1, x) + ends_half32 * ends(swap(diagonal(side, 2)), inside)
        field[W0, x + 2, ROWS, :] = jnp.where(has[side], b, 0.0)
    for r, own, sign, side in ((7, 8, -0.5, ym_side), (40, 39, 0.5, yp_side)):
        b = row_of_field(BP, r) + sign * row_of_field(U1, own)
        b = b + jnp.where(sub8 == 0, 0.5 * field[U0, 1, r : r + 1, :], 0.0)
        b = b - jnp.where(sub8 == 7, 0.5 * field[U0, 10, r : r + 1, :], 0.0)
        b = b + ends_half * ends_row(swap(diagonal(side, 1)), side[1])
        b = jnp.where(has[side], b, 0.0)
        for x in range(BX):
            field[W0, x + 2, r : r + 1, :] = b[x : x + 1]
    has_z = jnp.where(low_lane, has[zm_side].astype(jnp.float32), has[zp_side].astype(jnp.float32))

    def z_inside(t):
        return jnp.where(low_lane, turn(t, -1), turn(t, 1))

    def z_around_x(v, before, after):
        return (
            jnp.where(lane8 >= 112, turn(after, -16), turn(v, -16)),
            jnp.where(lane8 < 16, turn(before, 16), turn(v, 16)),
        )

    def z_around_y(v, before, after):
        up = jnp.where(y_group == 3, turn(after, 12), turn(v, -4))
        down = jnp.where(y_group == 0, turn(before, -12), turn(v, 4))
        return (
            turn(jnp.where(sub8 == 0, up, v), -1, 0),
            turn(jnp.where(sub8 == 7, down, v), 1, 0),
        )

    zero = jnp.zeros((8, BZ), jnp.float32)
    after, before = z_around_x(zero, diagonal(xm_side, 0), diagonal(xp_side, 0))
    b = pair(tlo[TB], thi[TB]) - 0.5 * (after - before)
    after, before = z_around_y(zero, diagonal(ym_side, 2), diagonal(yp_side, 2))
    b = b - 0.5 * (after - before) + jnp.where(low_lane, -0.5, 0.5) * z_inside(tz[TU2])
    s_w0 = swap(has_z * b)

    def operator(f, x, e):
        v = centre(f, x)
        yp, ym = around_y(f, x)
        zp, zm = around_z(v, e)
        out = cx[x + 2] * (v - centre(f, x + 1)) + cx[x + 1] * (v - centre(f, x - 1))
        out = out + (cy[x + 1, 1:33] * (v - yp) + cy[x + 1, 0:32] * (v - ym))
        return out + (czp[x + 1] * (v - zp) + czm[x + 1] * (v - zm))

    t_w = None
    for x in range(BX):
        out = operator(W0, x, ends(s_w0, x))
        field[W1, x + 2, ROWS, :] = out
        t_w = pack(out, t_w, x)
    tz[TW] = t_w
    send(IMAGE, XZ + YZ + XY)
    send(IMAGE, SIDES[:6])

    def fold(v):
        return (v[0:8] + v[8:16]) + (v[16:24] + v[24:32])

    def plus(acc, v):
        v = fold(v)
        return v if acc is None else acc + v

    m = [None] * 6
    for x in range(BX):
        v, out = centre(W0, x), centre(W1, x)
        m[0], m[1], m[2] = plus(m[0], v * v), plus(m[1], v * out), plus(m[2], out * out)
    for x, side, inside in ((-1, xm_side, 7), (BX, xp_side, 0)):
        c = centre(C, x)
        if x < 0:
            cx[0] = half * (c + centre(C, -2))
        else:
            cx[10] = half * (c + centre(C, 9))
        after, before = around_y(C, x)
        cy[x + 1, 0:32] = half * (c + before)
        cy[x + 1, 32:33] = half * (c[31:32] + after[31:32])
        after, before = around_z(c, ends(swap(diagonal(side, 1)), inside))
        czp[x + 1] = half * (c + after)
        czm[x + 1] = half * (c + before)
    z_edge = jnp.where(has[zm_side], 0.0, 1.0)
    y_edge = jnp.where(has[ym_side], 0.0, 1.0)
    x_edge = jnp.where(has[xm_side], 0.0, 1.0)
    for x in range(BX):
        low = jnp.where(first, czm[x + 1], 0.0) * z_edge
        low = low + jnp.where(row32 == 0, cy[x + 1, 0:32], 0.0) * y_edge
        if x == 0:
            low = low + cx[1] * x_edge
        zlow[x] = low

    receive(IMAGE)
    s_w1 = swap(pair(tlo[TW], thi[TW]))
    for x in range(BX):
        out = operator(W1, x, ends(s_w1, x))
        field[W2, x + 2, ROWS, :] = out
        v = centre(W1, x)
        m[3], m[4] = plus(m[3], v * out), plus(m[4], out * out)

    def image_plane(x, side, inside):
        out = operator(W1, x, ends(swap(diagonal(side, 3)), inside))
        field[W2, x + 2, ROWS, :] = jnp.where(has[side], out, 0.0)

    def image_row(r, beyond, own, side):
        sums = []
        c, v = row_of_field(C, r), row_of_field(W1, r)

        def term(cn, vn):
            return (c + cn) * (v - vn)

        out = term(row_of_field(C, beyond), row_of_field(W1, beyond)) + term(row_of_field(C, own), row_of_field(W1, own))
        both = []
        for f, q, values in ((C, 0, c), (W1, 3, v)):
            after = jnp.where(sub8 == 7, field[f, 10, r : r + 1, :], turn(values, -1, 0))
            before = jnp.where(sub8 == 0, field[f, 1, r : r + 1, :], turn(values, 1, 0))
            zp, zm = around_z(values, ends_row(swap(diagonal(side, q)), side[1]))
            both.append((after, before, zp, zm))
        for cn, vn in zip(*both):
            out = out + term(cn, vn)
        out = jnp.where(has[side], half * out, 0.0)
        for x in range(BX):
            field[W2, x + 2, r : r + 1, :] = out[x : x + 1]

    def image_face():
        both = []
        for t, qx, qy in ((TC, 1, 0), (TW, 3, 3)):
            lo, hi, own = tlo[t], thi[t], tz[t]
            v = pair(lo, hi)
            outer = jnp.where(low_lane, turn(lo, 1), turn(hi, -1))
            both.append(
                (v, outer, z_inside(own))
                + z_around_x(v, diagonal(xm_side, qx), diagonal(xp_side, qx))
                + z_around_y(v, diagonal(ym_side, qy), diagonal(yp_side, qy))
            )
        (c, *near_c), (v, *near_v) = both
        out = zero
        for cn, vn in zip(near_c, near_v):
            out = out + (c + cn) * (v - vn)
        return swap(has_z * (half * out))

    image_plane(BX, xp_side, 0)
    image_row(40, 41, 39, yp_side)
    s_w2 = image_face()
    for x in range(BX):
        v = centre(W2, x)
        dx = v - centre(W2, x + 1)
        dy = v - field[W2, x + 2, 9:41, :]
        dz_ = v - jnp.where(last, ends(s_w2, x), turn(v, -1))
        m[5] = plus(
            m[5],
            (cx[x + 2] * (dx * dx) + cy[x + 1, 1:33] * (dy * dy)) + (czp[x + 1] * (dz_ * dz_) + zlow[x] * (v * v)),
        )

    row = jnp.zeros((1, BZ), jnp.float32)
    for i in range(6):
        row = jnp.where(lane8[0:1] == i, jnp.sum(m[i], keepdims=True), row)

    def start_sum(phase, row, group):
        reduce[phase, 0:1, :] = row
        started = []
        for slot, partner in enumerate(group):
            copy = pltpu.make_async_remote_copy(
                src_ref=reduce.at[phase, pl.ds(0, 1)], dst_ref=reduce.at[phase, pl.ds(slot + 1, 1)],
                send_sem=sum_send.at[phase, slot], recv_sem=sum_recv.at[phase, slot],
                device_id=partner, device_id_type=MESH,
            )
            copy.start()
            started.append(copy)
        return started

    def end_sum(phase, started):
        for copy in started:
            copy.wait_recv()
        return row_total(reduce[phase])

    sums0 = start_sum(0, row, plane)
    image_plane(-1, xm_side, 7)
    image_row(7, 6, 8, ym_side)
    copy_u = pltpu.make_async_copy(field.at[(pl.ds(U0, 3),) + inner], u_out, copy_sem.at[0])
    copy_u.start()
    copy_w = pltpu.make_async_copy(field.at[(pl.ds(W0, 3),) + inner], w_out, copy_sem.at[1])
    copy_w.start()
    for i, (f, swapped) in enumerate(((W0, s_w0), (W1, s_w1), (W2, s_w2))):
        for x in range(BX):
            c = (0.5 / SCALE) * centre(C, x)
            g_out[i, 0, x] = c * (centre(f, x + 1) - centre(f, x - 1))
            after, before = around_y(f, x)
            g_out[i, 1, x] = c * (after - before)
            after, before = around_z(centre(f, x), ends(swapped, x))
            g_out[i, 2, x] = c * (after - before)
    receive(ENTH)
    s_h = swap(pair(tlo[TH], thi[TH]))
    for x in range(BX):
        h = centre(H, x)
        hyp, hym = around_y(H, x)
        hzp, hzm = around_z(h, ends(s_h, x))
        laplace = centre(H, x + 1) + centre(H, x - 1) + hyp + hym + hzp + hzm - 6.0 * h
        h_out[x] = h + DIFFUSE * laplace + HEATING * heat[x]
    copy_u.wait()
    copy_w.wait()
    for kind in range(4):
        for side in SIDES:
            if copies[kind][side]:

                @pl.when(has[side])
                def _():
                    for copy in copies[kind][side]:
                        copy.wait_send()

    high, low = end_sum(0, sums0)
    row = jnp.where(lane8 < 8, high, turn(low, 8))[0:1]
    sums1 = start_sum(1, row, column)
    high, low = end_sum(1, sums1)
    low = low + turn(high, -8)
    moments = [quick_sum(high[0:1, i : i + 1], low[0:1, i : i + 1]) for i in range(6)]
    for i, v in enumerate(solve_moments(moments)):
        c_out[i] = jnp.broadcast_to(v, (8, BZ))
    for copy in sums0 + sums1:
        copy.wait_send()


def finish(w, g, u, h, c, vel_out, p_out, h_out, vel, p, sem):
    copy_h = pltpu.make_async_copy(h, h_out, sem.at[0])
    copy_h.start()
    c0, c1, c2 = (jnp.concatenate([c[i]] * 4, axis=0) for i in range(3))
    copies = [copy_h]
    for i in range(3):
        for x in range(BX):
            vel[i, x] = u[i, x] - (c0 * g[0, i, x] + c1 * g[1, i, x] + c2 * g[2, i, x])
        copy = pltpu.make_async_copy(vel.at[i], vel_out.at[i], sem.at[1 + i])
        copy.start()
        copies.append(copy)
    scaled = tuple(v * (1.0 / SCALE) for v in (c0, c1, c2))
    for x in range(BX):
        p[x] = scaled[0] * w[0, x] + scaled[1] * w[1, x] + scaled[2] * w[2, x]
    copy_p = pltpu.make_async_copy(p, p_out, sem.at[4])
    copy_p.start()
    for copy in copies + [copy_p]:
        copy.wait()


def shards(*args):
    block = (BX, BY, BZ)
    f32 = jnp.float32
    any_ref = pl.BlockSpec(memory_space=pl.ANY)
    vmem = pl.BlockSpec(memory_space=pltpu.VMEM)
    results = pl.pallas_call(
        kernel,
        out_shape=(
            jax.ShapeDtypeStruct((3,) + block, f32),
            jax.ShapeDtypeStruct((3, 3) + block, f32),
            jax.ShapeDtypeStruct((3,) + block, f32),
            jax.ShapeDtypeStruct(block, f32),
            jax.ShapeDtypeStruct((3, 8, BZ), f32),
        ),
        in_specs=[any_ref] * 7,
        out_specs=(vmem,) * 5,
        scratch_shapes=[
            pltpu.VMEM((FIELDS, BX + 4, BY + 16, BZ), f32),
            pltpu.VMEM((7, 8, BZ), f32),
            pltpu.VMEM((7, 8, BZ), f32),
            pltpu.VMEM((7, 8, BZ), f32),
            pltpu.VMEM((8, 4, 8, BZ), f32),
            pltpu.VMEM((BX + 3, BY, BZ), f32),
            pltpu.VMEM((BX + 2, BY + 8, BZ), f32),
            pltpu.VMEM((BX + 2, BY, BZ), f32),
            pltpu.VMEM((BX + 2, BY, BZ), f32),
            pltpu.VMEM(block, f32),
            pltpu.VMEM(block, f32),
            pltpu.VMEM((SLOTS, BZ), jnp.int32),
            pltpu.VMEM((SLOTS, BZ), jnp.int32),
            pltpu.VMEM((SLOTS, BZ), jnp.int32),
            pltpu.VMEM((BX * BY, SLOTS * BZ), jnp.bfloat16),
            pltpu.VMEM((BZ, SLOTS * BZ), jnp.bfloat16),
            pltpu.VMEM((BX * BY, BZ), f32),
            pltpu.VMEM(block, f32),
            pltpu.VMEM((2, 16, BZ), f32),
            pltpu.SemaphoreType.DMA((7,)),
            pltpu.SemaphoreType.DMA((2,)),
            pltpu.SemaphoreType.DMA((N_MESSAGES,)),
            pltpu.SemaphoreType.DMA((N_MESSAGES,)),
            pltpu.SemaphoreType.DMA((2, 15)),
            pltpu.SemaphoreType.DMA((2, 15)),
        ],
        compiler_params=pltpu.CompilerParams(
            collective_id=0, has_side_effects=True, vmem_limit_bytes=32 * 1024 * 1024
        ),
        name="simple_step",
    )(*[pltpu.with_memory_space_constraint(a, pltpu.HBM) for a in args])
    results = [pltpu.with_memory_space_constraint(r, pltpu.VMEM) for r in results]
    return tuple(
        pl.pallas_call(
            finish,
            out_shape=(
                jax.ShapeDtypeStruct((3,) + block, f32),
                jax.ShapeDtypeStruct(block, f32),
                jax.ShapeDtypeStruct(block, f32),
            ),
            in_specs=[vmem] * 5,
            out_specs=(pl.BlockSpec(memory_space=pltpu.HBM),) * 3,
            scratch_shapes=[
                pltpu.VMEM((3,) + block, f32),
                pltpu.VMEM(block, f32),
                pltpu.SemaphoreType.DMA((5,)),
            ],
            compiler_params=pltpu.CompilerParams(vmem_limit_bytes=8 * 1024 * 1024),
            name="finish",
        )(*results)
    )


def solution(mesh):
    in_specs = (
        P(None, "gx", "gy", "gz"),
        P("gx", "gy", "gz"),
        P("gx", "gy", "gz"),
        P("gx", "gy", "gz"),
        P(("gx", "gy", "gz"), None),
        P(("gx", "gy", "gz"), None),
        P(("gx", "gy", "gz"), None),
    )
    out_specs = (P(None, "gx", "gy", "gz"), P("gx", "gy", "gz"), P("gx", "gy", "gz"))
    return jax.shard_map(shards, mesh=mesh, in_specs=in_specs, out_specs=out_specs, check_vma=False)
```

time: 46 us -> 33.5 us (0.73)
  local copies, waits for them, and re-layouts: 7.85 us -> 0 us
  Pallas kernels: 37.2 us -> 32.7 us
    unnamed x17 -> x0, local copies, waits for them, and re-layouts: 7.85 us -> none
    pallas_call x1, Pallas kernels: 37.2 us -> 31.8 us  [shards(): pl.pallas_call(kernel, out_shape=(jax.ShapeDtypeStruct((3,) + block, f32)...]
    pallas_call x0 -> x1, Pallas kernels: none -> 0.87 us  [shards(): pl.pallas_call(finish, out_shape=(jax.ShapeDtypeStruct((3,) + block, f32)...]
where the time goes in v2:
time: 33.5 us; the launch traced here: 33.3 us
  Pallas kernels  32.7 us (98%)
  between operations  0.64 us (2%)
    pallas_call x1, Pallas kernels, shards(): pl.pallas_call(kernel, out_shape=(jax.ShapeDtypeStruct((3,) + block, f32)...  31.8 us
    pallas_call x1, Pallas kernels, shards(): pl.pallas_call(finish, out_shape=(jax.ShapeDtypeStruct((3,) + block, f32)...  0.87 us

profile of v2, /device:TPU:1, one launch (start us, length us, event | category | flops | bytes accessed | tf_op | source)
XLA Modules:
  0.0 33.3 jit_solution(13597181981473860060)
XLA Ops:
  0.6 31.8 %simple_step.1 = (f32[3,8,32,128]{3,2,1,0:T(8,128)S(1)}, f32[3,3,8,32,128]{4,3,2,1,0:T(8,128)S(1)}, f32[3,8,32,128]{3,2,1,0:T(8,128)S(1)}, f32[8,32,128]{2,1,0:T(8,128)S(1)}, f32[3,8,128]{2,1,0:T(8,128)S(1)}) custom-call(f32[3,8,32,128]{3,2,1,0:T(8,128)} %vel.1, f32[8,32,128]{2,1,0:T(8,128)} %coef.1, f32[8,32,128]{2,1,0:T(8,128)} %enth.1, ...), custom_call_target="tpu_custom_call" | custom-call | tf_op jit(solution)/shard_map/simple_step/pallas_call | solution.py:661
  32.4 0.9 %finish.1 = (f32[3,8,32,128]{3,2,1,0:T(8,128)}, f32[8,32,128]{2,1,0:T(8,128)}, f32[8,32,128]{2,1,0:T(8,128)}) custom-call(f32[3,8,32,128]{3,2,1,0:T(8,128)S(1)} %get-tuple-element.8.w, f32[3,3,8,32,128]{4,3,2,1,0:T(8,128)S(1)} %get-tuple-element.9.g, f32[3,8,32,128]{3,2,1,0:T(8,128)S(1)} %get-tuple-element.10.u, f32[8,32,128]{2,1,0:T(8,128)S(1)} %get-tuple-element.11.h, ...), custom_call_target="tpu_custom_call" | custom-call | tf_op jit(solution)/shard_map/finish/pallas_call | solution.py:706

commit v3 on v2

--- a/solution.py
+++ b/solution.py
@@ -1,3 +1,5 @@
+import math
+
 import jax
 import jax.numpy as jnp
 from jax import lax
@@ -13,16 +15,16 @@
 HEATING = 0.5
 EXPANSION = 1.5
 SCALE = 16.0
-H, C, U0, U1, U2, BP, W0, W1, W2 = range(9)
+H, C, U0, BP, U1, U2, W0, W1, W2 = range(9)
 FIELDS = 9
-TU0, TC, TU2, TU1, TH, TB, TW = range(7)
+TU0, TC, TU2, TB, TU1, TH, TW = range(7)
 ROWS = slice(8, 40)
 SIGNS = (-1, 1)
 XZ = tuple((a, 0, c) for a in SIGNS for c in SIGNS)
 YZ = tuple((0, b, c) for b in SIGNS for c in SIGNS)
 XY = tuple((a, b, 0) for a in SIGNS for b in SIGNS)
 SIDES = ((-1, 0, 0), (1, 0, 0), (0, -1, 0), (0, 1, 0), (0, 0, -1), (0, 0, 1)) + XY + XZ + YZ
-EARLY, LATE, ENTH, IMAGE = range(4)
+FIRST, ENTH, IMAGE = range(3)
 PIVOT_FLOOR = 1e-9
 
 
@@ -60,32 +62,37 @@
     return quick_sum(p, e + (a[0] * b[1] + a[1] * b[0]))
 
 
-def df_div(a, b):
-    q = a[0] / b[0]
+def df_over(a, b, inverse):
+    q = a[0] * inverse
     p, e = two_mul(q, b[0])
-    rest = ((a[0] - p) - e) + a[1] - q * b[1]
-    return quick_sum(q, rest / b[0])
+    rest = ((a[0] - p) - e) + (a[1] - q * b[1])
+    return quick_sum(q, rest * inverse)
 
 
 def solve_moments(m):
-    l10 = df_div(m[2], m[1])
-    l20 = df_div(m[3], m[1])
+    i0 = 1.0 / m[1][0]
+    l10 = df_over(m[2], m[1], i0)
+    l20 = df_over(m[3], m[1], i0)
     d1 = df_sub(m[3], df_mul(l10, m[2]))
     e12 = df_sub(m[4], df_mul(l10, m[3]))
     y1 = df_sub(m[1], df_mul(l10, m[0]))
     y2 = df_sub(m[2], df_mul(l20, m[0]))
     d2 = df_sub(m[5], df_mul(l20, m[3]))
     ok1 = d1[0] > PIVOT_FLOOR * m[3][0]
-    l21 = df_div(e12, d1)
-    l21 = tuple(jnp.where(ok1, v, 0.0) for v in l21)
+    i1 = jnp.where(ok1, 1.0 / d1[0], 0.0)
+    l21 = df_over(e12, d1, i1)
     d2 = df_sub(d2, df_mul(l21, e12))
     y2 = df_sub(y2, df_mul(l21, y1))
     ok2 = ok1 & (d2[0] > PIVOT_FLOOR * m[5][0])
-    c2 = tuple(jnp.where(ok2, v, 0.0) for v in df_div(y2, d2))
-    c1 = tuple(jnp.where(ok1, v, 0.0) for v in df_div(y1, d1))
-    c1 = df_sub(c1, df_mul(l21, c2))
-    c0 = df_sub(df_sub(df_div(m[0], m[1]), df_mul(l10, c1)), df_mul(l20, c2))
-    return c0[0], c1[0], c2[0]
+    c2 = jnp.where(ok2, y2[0] / d2[0], 0.0)
+    p, e = two_mul(e12[0], c2)
+    c1 = (((y1[0] - p) - e) + (y1[1] - e12[1] * c2)) * i1
+    p1, e1 = two_mul(m[2][0], c1)
+    p2, e2 = two_mul(m[3][0], c2)
+    s, t1 = two_sum(m[0][0], -p1)
+    s, t2 = two_sum(s, -p2)
+    rest = (t1 - e1) + (t2 - e2) + (m[0][1] - m[2][1] * c1 - m[3][1] * c2)
+    return (s + rest) * i0, c1, c2
 
 
 def row_total(rows):
@@ -108,70 +115,60 @@
     xs2, xd2 = {-1: pl.ds(2, 2), 1: pl.ds(8, 2)}, {-1: pl.ds(10, 2), 1: pl.ds(0, 2)}
     ys2, yd2 = {-1: pl.ds(8, 2), 1: pl.ds(38, 2)}, {-1: pl.ds(40, 2), 1: pl.ds(6, 2)}
     rows, planes = pl.ds(8, BY), pl.ds(2, BX)
-    table = [{}, {}, {}, {}]
-    for side in SIDES:
+    table = [[], [], []]
+    for side in XZ + YZ + XY + SIDES[:2] + SIDES[4:6] + SIDES[2:4]:
         a, b, c = side
         far = thi if c < 0 else tlo
         slot = (XZ + YZ).index(opposite(side)) if side in XZ + YZ else None
+        enth = []
         if side in XZ:
-            early = [(tz.at[pl.ds(TU0, 3)], dz.at[slot, pl.ds(0, 3)])]
-            image = [(tz.at[TW], dz.at[slot, 3])]
-            late = enth = []
+            first = [(tz.at[pl.ds(TU0, 3)], dz.at[slot, pl.ds(0, 3)])]
+            image = [(tz.at[TW], dz.at[slot, 4])]
         elif side in YZ:
-            early = [(tz.at[pl.ds(TC, 3)], dz.at[slot, pl.ds(0, 3)])]
-            image = [(tz.at[TW], dz.at[slot, 3])]
-            late = enth = []
+            first = [(tz.at[pl.ds(TC, 4)], dz.at[slot, pl.ds(0, 4)])]
+            image = [(tz.at[TW], dz.at[slot, 4])]
         elif side in XY:
-            early = [(field.at[pl.ds(C, 3), xs[a], ys[b]], field.at[pl.ds(C, 3), xd[a], yd[b]])]
+            first = [(field.at[pl.ds(C, 4), xs[a], ys[b]], field.at[pl.ds(C, 4), xd[a], yd[b]])]
             image = [(field.at[W1, xs[a], ys[b]], field.at[W1, xd[a], yd[b]])]
-            late = enth = []
         elif a:
-            early = [
+            first = [
                 (field.at[C, xs2[a], rows], field.at[C, xd2[a], rows]),
-                (field.at[U0, xs[a], rows], field.at[U0, xd[a], rows]),
+                (field.at[pl.ds(U0, 2), xs[a], rows], field.at[pl.ds(U0, 2), xd[a], rows]),
             ]
-            late = [(field.at[BP, xs[a], rows], field.at[BP, xd[a], rows])]
             enth = [(field.at[H, xs[a], rows], field.at[H, xd[a], rows])]
             image = [(field.at[W1, xs2[a], rows], field.at[W1, xd2[a], rows])]
         elif b:
-            early = [
+            first = [
                 (field.at[C, planes, ys2[b]], field.at[C, planes, yd2[b]]),
-                (field.at[U1, planes, ys[b]], field.at[U1, planes, yd[b]]),
+                (field.at[pl.ds(BP, 2), planes, ys[b]], field.at[pl.ds(BP, 2), planes, yd[b]]),
             ]
-            late = [(field.at[BP, planes, ys[b]], field.at[BP, planes, yd[b]])]
             enth = [(field.at[H, planes, ys[b]], field.at[H, planes, yd[b]])]
             image = [(field.at[W1, planes, ys2[b]], field.at[W1, planes, yd2[b]])]
         else:
-            early = [(tz.at[pl.ds(TC, 2)], far.at[pl.ds(TC, 2)])]
-            late = [(tz.at[TB], far.at[TB])]
+            first = [(tz.at[pl.ds(TC, 3)], far.at[pl.ds(TC, 3)])]
             enth = [(tz.at[TH], far.at[TH])]
             image = [(tz.at[TW], far.at[TW])]
-        for kind, pairs in ((EARLY, early), (LATE, late), (ENTH, enth), (IMAGE, image)):
-            table[kind][side] = pairs
+        for kind, pairs in ((FIRST, first), (ENTH, enth), (IMAGE, image)):
+            table[kind] += [(side, src, dst) for src, dst in pairs]
     return table
-
-
-N_MESSAGES = 22 + 6 + 6 + 18
 
 
 def kernel(
     vel, coef, enth, void, cells, normal, flag,
     w_out, g_out, u_out, h_out, c_out,
     field, tz, tlo, thi, dz, cx, cy, czm, czp, zlow, av, wc, wn, wf, hot_row, hot_lane, grid,
-    heat, reduce, load_sem, copy_sem, send_sem, recv_sem, sum_send, sum_recv,
+    heat, reduce, tally, load_sem, copy_sem, send_sem, recv_sem, sum_send, sum_recv,
 ):
     gx, gy, gz = lax.axis_index("gx"), lax.axis_index("gy"), lax.axis_index("gz")
     chip_y, core = gy // 2, lax.rem(gy, 2)
 
-    def exists(side):
-        found = None
-        for at, step, size in zip((gx, gy, gz), side, (NGX, NGY, NGZ)):
-            if step:
-                inside = at > 0 if step < 0 else at < size - 1
-                found = inside if found is None else found & inside
-        return found
-
-    has = {side: exists(side) for side in SIDES}
+    has = dict(zip(SIDES[:6], (gx > 0, gx < NGX - 1, gy > 0, gy < NGY - 1, gz > 0, gz < NGZ - 1)))
+
+    def beside(side):
+        return tuple(
+            lax.rem(at + step + size, size) if step else at
+            for at, step, size in zip((gx, gy, gz), side, (NGX, NGY, NGZ))
+        )
 
     def in_plane(i, j):
         return (lax.rem(gx + i, NGX), lax.rem(chip_y + j, NGY // 2) * 2 + core, gz)
@@ -188,7 +185,8 @@
     inner = (pl.ds(2, BX), pl.ds(8, BY))
     loads = [
         (cells, wc), (flag, wf), (normal, wn),
-        (vel, field.at[(pl.ds(U0, 3),) + inner]),
+        (vel.at[0], field.at[(U0,) + inner]),
+        (vel.at[pl.ds(1, 2)], field.at[(pl.ds(U1, 2),) + inner]),
         (void, av),
         (coef, field.at[(C,) + inner]),
         (enth, field.at[(H,) + inner]),
@@ -198,63 +196,44 @@
         copy.start()
 
     barrier = pltpu.get_barrier_semaphore()
-    for partner in column + plane:
+    greeted = [beside(side) for side in SIDES] + plane[::-1] + column[::-1]
+    for partner in greeted:
         pl.semaphore_signal(barrier, inc=1, device_id=partner, device_id_type=MESH)
-    expected = len(plane) + len(column)
-    for side in SIDES:
-        a, b, c = side
-        if (a and not b and not c) or (c and not a and not b):
-            continue
-        met = has[side]
-        if b and not a:
-            met = met & (core == (0 if b < 0 else 1))
-
-        @pl.when(met)
-        def _():
-            pl.semaphore_signal(barrier, inc=1, device_id=(gx + a, gy + b, gz + c), device_id_type=MESH)
-
-        expected = expected + met.astype(jnp.int32)
 
     table = messages(field, tz, tlo, thi, dz)
-    copies = [{}, {}, {}, {}]
-    at = 0
-    for kind in range(4):
-        for side in SIDES:
-            copies[kind][side] = []
-            for src, dst in table[kind][side]:
-                copies[kind][side].append(
-                    pltpu.make_async_remote_copy(
-                        src_ref=src, dst_ref=dst, send_sem=send_sem.at[at], recv_sem=recv_sem.at[at],
-                        device_id=(gx + side[0], gy + side[1], gz + side[2]), device_id_type=MESH,
-                    )
-                )
-                at += 1
-
-    def send(kind, sides):
-        for side in sides:
-            if copies[kind][side]:
-
-                @pl.when(has[side])
-                def _():
-                    for copy in copies[kind][side]:
-                        copy.start()
+    copies = [
+        [
+            pltpu.make_async_remote_copy(
+                src_ref=src, dst_ref=dst, send_sem=send_sem.at[kind], recv_sem=recv_sem.at[kind],
+                device_id=beside(side), device_id_type=MESH,
+            )
+            for side, src, dst in table[kind]
+        ]
+        for kind in range(3)
+    ]
+
+    def whole(kind):
+        count = sum(math.prod(dst.shape) for _, _, dst in table[kind]) // BZ
+        ref = tally.at[pl.ds(0, count)]
+        return pltpu.make_async_remote_copy(
+            src_ref=ref, dst_ref=ref, send_sem=send_sem.at[kind], recv_sem=recv_sem.at[kind],
+            device_id=beside(SIDES[0]), device_id_type=MESH,
+        )
+
+    def send(kind):
+        for copy in copies[kind]:
+            copy.start()
 
     def receive(kind):
-        for side in SIDES:
-            if copies[kind][side]:
-
-                @pl.when(has[opposite(side)])
-                def _():
-                    for copy in copies[kind][side]:
-                        copy.wait_recv()
-
-    for side in SIDES:
-
-        @pl.when(jnp.logical_not(has[opposite(side)]))
-        def _():
-            for kind in range(4):
-                for _, dst in table[kind][side]:
-                    dst[...] = jnp.zeros(dst.shape, jnp.float32)
+        whole(kind).wait_recv()
+        for side in SIDES[:6]:
+            dim = [i for i in range(3) if side[i]][0]
+
+            @pl.when(jnp.logical_not(has[side]))
+            def _():
+                for to, _, dst in table[kind]:
+                    if to[dim] == -side[dim]:
+                        dst[...] = jnp.zeros(dst.shape, jnp.float32)
 
     lane8 = lax.broadcasted_iota(jnp.int32, (8, BZ), 1)
     sub8 = lax.broadcasted_iota(jnp.int32, (8, BZ), 0)
@@ -368,10 +347,8 @@
     for i, t in ((TB, t_b), (TC, t_c), (TU0, t_u0), (TU1, t_u1), (TU2, t_u2)):
         tz[i] = t
 
-    pl.semaphore_wait(barrier, expected)
-    send(EARLY, XZ + YZ + XY)
-    send(EARLY, SIDES[:6])
-    send(LATE, SIDES[:6])
+    pl.semaphore_wait(barrier, len(greeted))
+    send(FIRST)
 
     t_h = None
     half = 0.5 / SCALE
@@ -384,7 +361,7 @@
         czp[x + 1] = half * jnp.where(last, c, c + turn(c, -1))
         czm[x + 1] = half * jnp.where(first, c, c + turn(c, 1))
     tz[TH] = t_h
-    send(ENTH, SIDES[:6])
+    send(ENTH)
 
     def low_high(v):
         return v[0:8], v[8:24], v[24:32]
@@ -395,8 +372,7 @@
         z = z - jnp.where(sub8 == 7, 0.5 * field[f, x + 2, 40:41, :], 0.0)
         return jnp.concatenate([a, m, z], axis=0)
 
-    receive(EARLY)
-    receive(LATE)
+    receive(FIRST)
     s_u2 = swap(pair(tlo[TU2], thi[TU2]))
     s_c = swap(pair(tlo[TC], thi[TC]))
     for x in range(BX):
@@ -449,7 +425,7 @@
     zero = jnp.zeros((8, BZ), jnp.float32)
     after, before = z_around_x(zero, diagonal(xm_side, 0), diagonal(xp_side, 0))
     b = pair(tlo[TB], thi[TB]) - 0.5 * (after - before)
-    after, before = z_around_y(zero, diagonal(ym_side, 2), diagonal(yp_side, 2))
+    after, before = z_around_y(zero, diagonal(ym_side, 3), diagonal(yp_side, 3))
     b = b - 0.5 * (after - before) + jnp.where(low_lane, -0.5, 0.5) * z_inside(tz[TU2])
     s_w0 = swap(has_z * b)
 
@@ -467,8 +443,7 @@
         field[W1, x + 2, ROWS, :] = out
         t_w = pack(out, t_w, x)
     tz[TW] = t_w
-    send(IMAGE, XZ + YZ + XY)
-    send(IMAGE, SIDES[:6])
+    send(IMAGE)
 
     def fold(v):
         return (v[0:8] + v[8:16]) + (v[16:24] + v[24:32])
@@ -512,7 +487,7 @@
         m[3], m[4] = plus(m[3], v * out), plus(m[4], out * out)
 
     def image_plane(x, side, inside):
-        out = operator(W1, x, ends(swap(diagonal(side, 3)), inside))
+        out = operator(W1, x, ends(swap(diagonal(side, 4)), inside))
         field[W2, x + 2, ROWS, :] = jnp.where(has[side], out, 0.0)
 
     def image_row(r, beyond, own, side):
@@ -524,7 +499,7 @@
 
         out = term(row_of_field(C, beyond), row_of_field(W1, beyond)) + term(row_of_field(C, own), row_of_field(W1, own))
         both = []
-        for f, q, values in ((C, 0, c), (W1, 3, v)):
+        for f, q, values in ((C, 0, c), (W1, 4, v)):
             after = jnp.where(sub8 == 7, field[f, 10, r : r + 1, :], turn(values, -1, 0))
             before = jnp.where(sub8 == 0, field[f, 1, r : r + 1, :], turn(values, 1, 0))
             zp, zm = around_z(values, ends_row(swap(diagonal(side, q)), side[1]))
@@ -537,7 +512,7 @@
 
     def image_face():
         both = []
-        for t, qx, qy in ((TC, 1, 0), (TW, 3, 3)):
+        for t, qx, qy in ((TC, 1, 0), (TW, 4, 4)):
             lo, hi, own = tlo[t], thi[t], tz[t]
             v = pair(lo, hi)
             outer = jnp.where(low_lane, turn(lo, 1), turn(hi, -1))
@@ -569,29 +544,35 @@
     for i in range(6):
         row = jnp.where(lane8[0:1] == i, jnp.sum(m[i], keepdims=True), row)
 
+    def sum_copy(phase, slot, partner):
+        return pltpu.make_async_remote_copy(
+            src_ref=reduce.at[phase, pl.ds(0, 1)], dst_ref=reduce.at[phase, pl.ds(slot + 1, 1)],
+            send_sem=sum_send.at[phase], recv_sem=sum_recv.at[phase], device_id=partner, device_id_type=MESH,
+        )
+
+    def sum_whole(phase):
+        ref = tally.at[pl.ds(0, 15)]
+        return pltpu.make_async_remote_copy(
+            src_ref=ref, dst_ref=ref, send_sem=sum_send.at[phase], recv_sem=sum_recv.at[phase],
+            device_id=plane[0], device_id_type=MESH,
+        )
+
     def start_sum(phase, row, group):
         reduce[phase, 0:1, :] = row
-        started = []
         for slot, partner in enumerate(group):
-            copy = pltpu.make_async_remote_copy(
-                src_ref=reduce.at[phase, pl.ds(0, 1)], dst_ref=reduce.at[phase, pl.ds(slot + 1, 1)],
-                send_sem=sum_send.at[phase, slot], recv_sem=sum_recv.at[phase, slot],
-                device_id=partner, device_id_type=MESH,
-            )
-            copy.start()
-            started.append(copy)
-        return started
-
-    def end_sum(phase, started):
-        for copy in started:
-            copy.wait_recv()
+            sum_copy(phase, slot, partner).start()
+
+    def end_sum(phase):
+        sum_whole(phase).wait_recv()
         return row_total(reduce[phase])
 
-    sums0 = start_sum(0, row, plane)
+    start_sum(0, row, plane)
     image_plane(-1, xm_side, 7)
     image_row(7, 6, 8, ym_side)
-    copy_u = pltpu.make_async_copy(field.at[(pl.ds(U0, 3),) + inner], u_out, copy_sem.at[0])
+    copy_u = pltpu.make_async_copy(field.at[(U0,) + inner], u_out.at[0], copy_sem.at[0])
     copy_u.start()
+    copy_v = pltpu.make_async_copy(field.at[(pl.ds(U1, 2),) + inner], u_out.at[pl.ds(1, 2)], copy_sem.at[2])
+    copy_v.start()
     copy_w = pltpu.make_async_copy(field.at[(pl.ds(W0, 3),) + inner], w_out, copy_sem.at[1])
     copy_w.start()
     for i, (f, swapped) in enumerate(((W0, s_w0), (W1, s_w1), (W2, s_w2))):
@@ -611,26 +592,26 @@
         laplace = centre(H, x + 1) + centre(H, x - 1) + hyp + hym + hzp + hzm - 6.0 * h
         h_out[x] = h + DIFFUSE * laplace + HEATING * heat[x]
     copy_u.wait()
+    copy_v.wait()
     copy_w.wait()
-    for kind in range(4):
-        for side in SIDES:
-            if copies[kind][side]:
-
-                @pl.when(has[side])
-                def _():
-                    for copy in copies[kind][side]:
-                        copy.wait_send()
-
-    high, low = end_sum(0, sums0)
+    for kind in range(3):
+        whole(kind).wait_send()
+
+    high, low = end_sum(0)
     row = jnp.where(lane8 < 8, high, turn(low, 8))[0:1]
-    sums1 = start_sum(1, row, column)
-    high, low = end_sum(1, sums1)
+    start_sum(1, row, column)
+    high, low = end_sum(1)
     low = low + turn(high, -8)
-    moments = [quick_sum(high[0:1, i : i + 1], low[0:1, i : i + 1]) for i in range(6)]
+    high, low = quick_sum(high, low)
+
+    def spread(v, i):
+        return jnp.broadcast_to(v[:, i : i + 1], (8, BZ))
+
+    moments = [(spread(high, i), spread(low, i)) for i in range(6)]
     for i, v in enumerate(solve_moments(moments)):
-        c_out[i] = jnp.broadcast_to(v, (8, BZ))
-    for copy in sums0 + sums1:
-        copy.wait_send()
+        c_out[i] = v
+    sum_whole(0).wait_send()
+    sum_whole(1).wait_send()
 
 
 def finish(w, g, u, h, c, vel_out, p_out, h_out, vel, p, sem):
@@ -674,7 +655,7 @@
             pltpu.VMEM((7, 8, BZ), f32),
             pltpu.VMEM((7, 8, BZ), f32),
             pltpu.VMEM((7, 8, BZ), f32),
-            pltpu.VMEM((8, 4, 8, BZ), f32),
+            pltpu.VMEM((8, 5, 8, BZ), f32),
             pltpu.VMEM((BX + 3, BY, BZ), f32),
             pltpu.VMEM((BX + 2, BY + 8, BZ), f32),
             pltpu.VMEM((BX + 2, BY, BZ), f32),
@@ -689,12 +670,13 @@
             pltpu.VMEM((BX * BY, BZ), f32),
             pltpu.VMEM(block, f32),
             pltpu.VMEM((2, 16, BZ), f32),
-            pltpu.SemaphoreType.DMA((7,)),
+            pltpu.VMEM((1024, BZ), f32),
+            pltpu.SemaphoreType.DMA((8,)),
+            pltpu.SemaphoreType.DMA((3,)),
+            pltpu.SemaphoreType.DMA((3,)),
+            pltpu.SemaphoreType.DMA((3,)),
             pltpu.SemaphoreType.DMA((2,)),
-            pltpu.SemaphoreType.DMA((N_MESSAGES,)),
-            pltpu.SemaphoreType.DMA((N_MESSAGES,)),
-            pltpu.SemaphoreType.DMA((2, 15)),
-            pltpu.SemaphoreType.DMA((2, 15)),
+            pltpu.SemaphoreType.DMA((2,)),
         ],
         compiler_params=pltpu.CompilerParams(
             collective_id=0, has_side_effects=True, vmem_limit_bytes=32 * 1024 * 1024

time: 33.5 us -> 32.2 us (0.961)
  Pallas kernels: 32.7 us -> 31.5 us
    pallas_call x1, Pallas kernels: 31.8 us -> 30.6 us  [shards(): pl.pallas_call(kernel, out_shape=(jax.ShapeDtypeStruct((3,) + block, f32)...]
where the time goes in v3:
time: 32.2 us; the launch traced here: 32.1 us
  Pallas kernels  31.5 us (98%)
  between operations  0.64 us (2%)
    pallas_call x1, Pallas kernels, shards(): pl.pallas_call(kernel, out_shape=(jax.ShapeDtypeStruct((3,) + block, f32)...  30.6 us
    pallas_call x1, Pallas kernels, shards(): pl.pallas_call(finish, out_shape=(jax.ShapeDtypeStruct((3,) + block, f32)...  0.87 us

profile of v3, /device:TPU:1, one launch (start us, length us, event | category | flops | bytes accessed | tf_op | source)
XLA Modules:
  0.0 32.1 jit_solution(4634469593950921896)
XLA Ops:
  0.6 30.6 %simple_step.1 = (f32[3,8,32,128]{3,2,1,0:T(8,128)S(1)}, f32[3,3,8,32,128]{4,3,2,1,0:T(8,128)S(1)}, f32[3,8,32,128]{3,2,1,0:T(8,128)S(1)}, f32[8,32,128]{2,1,0:T(8,128)S(1)}, f32[3,8,128]{2,1,0:T(8,128)S(1)}) custom-call(f32[3,8,32,128]{3,2,1,0:T(8,128)} %vel.1, f32[8,32,128]{2,1,0:T(8,128)} %coef.1, f32[8,32,128]{2,1,0:T(8,128)} %enth.1, ...), custom_call_target="tpu_custom_call" | custom-call | tf_op jit(solution)/shard_map/simple_step/pallas_call | solution.py:642
  31.2 0.9 %finish.1 = (f32[3,8,32,128]{3,2,1,0:T(8,128)}, f32[8,32,128]{2,1,0:T(8,128)}, f32[8,32,128]{2,1,0:T(8,128)}) custom-call(f32[3,8,32,128]{3,2,1,0:T(8,128)S(1)} %get-tuple-element.8.w, f32[3,3,8,32,128]{4,3,2,1,0:T(8,128)S(1)} %get-tuple-element.9.g, f32[3,8,32,128]{3,2,1,0:T(8,128)S(1)} %get-tuple-element.10.u, f32[8,32,128]{2,1,0:T(8,128)S(1)} %get-tuple-element.11.h, ...), custom_call_target="tpu_custom_call" | custom-call | tf_op jit(solution)/shard_map/finish/pallas_call | solution.py:688

commit v4 on v3

--- a/solution.py
+++ b/solution.py
@@ -26,6 +26,8 @@
 SIDES = ((-1, 0, 0), (1, 0, 0), (0, -1, 0), (0, 1, 0), (0, 0, -1), (0, 0, 1)) + XY + XZ + YZ
 FIRST, ENTH, IMAGE = range(3)
 PIVOT_FLOOR = 1e-9
+ROOT = (0, 1, 0)
+DEVICES = 256
 
 
 def two_sum(a, b):
@@ -96,7 +98,14 @@
 
 
 def row_total(rows):
-    s, e = two_sum(rows[0:8], rows[8:16])
+    parts = [(rows[i : i + 8], None) for i in range(0, rows.shape[0], 8)]
+    while len(parts) > 1:
+        merged = []
+        for (a, low_a), (b, low_b) in zip(parts[0::2], parts[1::2]):
+            s, e = two_sum(a, b)
+            merged.append((s, e if low_a is None else e + (low_a + low_b)))
+        parts = merged
+    s, e = parts[0]
     for step in (4, 2, 1):
         other = pltpu.roll(s, step, axis=0)
         e = e + pltpu.roll(e, step, axis=0)
@@ -157,7 +166,7 @@
     vel, coef, enth, void, cells, normal, flag,
     w_out, g_out, u_out, h_out, c_out,
     field, tz, tlo, thi, dz, cx, cy, czm, czp, zlow, av, wc, wn, wf, hot_row, hot_lane, grid,
-    heat, reduce, tally, load_sem, copy_sem, send_sem, recv_sem, sum_send, sum_recv,
+    heat, reduce, direct, total, tally, load_sem, copy_sem, send_sem, recv_sem, sum_send, sum_recv, ready,
 ):
     gx, gy, gz = lax.axis_index("gx"), lax.axis_index("gy"), lax.axis_index("gz")
     chip_y, core = gy // 2, lax.rem(gy, 2)
@@ -363,6 +372,16 @@
     tz[TH] = t_h
     send(ENTH)
 
+    in_root_plane = (gz == ROOT[2]) & (core == ROOT[1] % 2)
+    in_root_column = (gx == ROOT[0]) & (chip_y == ROOT[1] // 2)
+    is_root = in_root_plane & in_root_column
+
+    @pl.when(in_root_plane)
+    def _():
+        for partner in column:
+            pl.semaphore_signal(ready, inc=1, device_id=partner, device_id_type=MESH)
+
+
     def low_high(v):
         return v[0:8], v[8:24], v[24:32]
 
@@ -550,23 +569,30 @@
             send_sem=sum_send.at[phase], recv_sem=sum_recv.at[phase], device_id=partner, device_id_type=MESH,
         )
 
-    def sum_whole(phase):
-        ref = tally.at[pl.ds(0, 15)]
+    def sum_whole(phase, count):
+        ref = tally.at[pl.ds(0, count)]
         return pltpu.make_async_remote_copy(
             src_ref=ref, dst_ref=ref, send_sem=sum_send.at[phase], recv_sem=sum_recv.at[phase],
             device_id=plane[0], device_id_type=MESH,
         )
 
-    def start_sum(phase, row, group):
-        reduce[phase, 0:1, :] = row
+    def start_sum(phase, group):
         for slot, partner in enumerate(group):
             sum_copy(phase, slot, partner).start()
 
-    def end_sum(phase):
-        sum_whole(phase).wait_recv()
-        return row_total(reduce[phase])
-
-    start_sum(0, row, plane)
+    me = (gx * NGY + gy) * NGZ + gz
+    to_root = pltpu.make_async_remote_copy(
+        src_ref=reduce.at[0, pl.ds(0, 1)], dst_ref=direct.at[me], send_sem=sum_send.at[2],
+        recv_sem=sum_recv.at[2], device_id=ROOT, device_id_type=MESH,
+    )
+
+    @pl.when(jnp.logical_not(in_root_plane))
+    def _():
+        pl.semaphore_wait(ready, 1)
+
+    reduce[0, 0:1, :] = row
+    pl.when(jnp.logical_not(is_root))(to_root.start)
+    start_sum(0, plane)
     image_plane(-1, xm_side, 7)
     image_row(7, 6, 8, ym_side)
     copy_u = pltpu.make_async_copy(field.at[(U0,) + inner], u_out.at[0], copy_sem.at[0])
@@ -597,11 +623,35 @@
     for kind in range(3):
         whole(kind).wait_send()
 
-    high, low = end_sum(0)
-    row = jnp.where(lane8 < 8, high, turn(low, 8))[0:1]
-    start_sum(1, row, column)
-    high, low = end_sum(1)
-    low = low + turn(high, -8)
+    sum_whole(0, 15).wait_recv()
+    high, low = row_total(reduce[0])
+    reduce[1, 0:1, :] = jnp.where(lane8 < 8, high, turn(low, 8))[0:1]
+
+    @pl.when(jnp.logical_not(in_root_column) | is_root)
+    def _():
+        start_sum(1, column)
+
+    @pl.when(in_root_column & jnp.logical_not(is_root))
+    def _():
+        for slot, partner in enumerate(column):
+            pl.when((partner[1] != ROOT[1]) | (partner[2] != ROOT[2]))(sum_copy(1, slot, partner).start)
+
+    @pl.when(is_root)
+    def _():
+        direct[(ROOT[0] * NGY + ROOT[1]) * NGZ + ROOT[2]] = row
+        sum_whole(2, DEVICES - 1).wait_recv()
+        high, low = row_total(direct[...].reshape(DEVICES, BZ))
+        total[0] = high
+        total[1] = low
+
+    @pl.when(jnp.logical_not(is_root))
+    def _():
+        sum_whole(1, 15).wait_recv()
+        high, low = row_total(reduce[1])
+        total[0] = high
+        total[1] = low + turn(high, -8)
+
+    high, low = total[0], total[1]
     high, low = quick_sum(high, low)
 
     def spread(v, i):
@@ -610,8 +660,17 @@
     moments = [(spread(high, i), spread(low, i)) for i in range(6)]
     for i, v in enumerate(solve_moments(moments)):
         c_out[i] = v
-    sum_whole(0).wait_send()
-    sum_whole(1).wait_send()
+    sum_whole(0, 15).wait_send()
+
+    @pl.when(in_root_column & jnp.logical_not(is_root))
+    def _():
+        sum_whole(1, 14).wait_send()
+
+    @pl.when(jnp.logical_not(in_root_column) | is_root)
+    def _():
+        sum_whole(1, 15).wait_send()
+
+    pl.when(jnp.logical_not(is_root))(to_root.wait_send)
 
 
 def finish(w, g, u, h, c, vel_out, p_out, h_out, vel, p, sem):
@@ -670,13 +729,16 @@
             pltpu.VMEM((BX * BY, BZ), f32),
             pltpu.VMEM(block, f32),
             pltpu.VMEM((2, 16, BZ), f32),
+            pltpu.VMEM((DEVICES, 1, BZ), f32),
+            pltpu.VMEM((2, 8, BZ), f32),
             pltpu.VMEM((1024, BZ), f32),
             pltpu.SemaphoreType.DMA((8,)),
             pltpu.SemaphoreType.DMA((3,)),
             pltpu.SemaphoreType.DMA((3,)),
             pltpu.SemaphoreType.DMA((3,)),
-            pltpu.SemaphoreType.DMA((2,)),
-            pltpu.SemaphoreType.DMA((2,)),
+            pltpu.SemaphoreType.DMA((3,)),
+            pltpu.SemaphoreType.DMA((3,)),
+            pltpu.SemaphoreType.REGULAR,
         ],
         compiler_params=pltpu.CompilerParams(
             collective_id=0, has_side_effects=True, vmem_limit_bytes=32 * 1024 * 1024

time: 32.2 us -> 30.8 us (0.957)
  the two profiles are of different devices: /device:TPU:1 before, /device:TPU:2 now
where the time goes in v4:
time: 30.8 us; the launch traced here: 30.7 us
  Pallas kernels  30.1 us (98%)
  between operations  0.64 us (2%)
    pallas_call x1, Pallas kernels, shards(): pl.pallas_call(kernel, out_shape=(jax.ShapeDtypeStruct((3,) + block, f32)...  29.2 us
    pallas_call x1, Pallas kernels, shards(): pl.pallas_call(finish, out_shape=(jax.ShapeDtypeStruct((3,) + block, f32)...  0.87 us

profile of v4, /device:TPU:2, one launch (start us, length us, event | category | flops | bytes accessed | tf_op | source)
XLA Modules:
  0.0 30.7 jit_solution(15088761925633080130)
XLA Ops:
  0.6 29.2 %simple_step.1 = (f32[3,8,32,128]{3,2,1,0:T(8,128)S(1)}, f32[3,3,8,32,128]{4,3,2,1,0:T(8,128)S(1)}, f32[3,8,32,128]{3,2,1,0:T(8,128)S(1)}, f32[8,32,128]{2,1,0:T(8,128)S(1)}, f32[3,8,128]{2,1,0:T(8,128)S(1)}) custom-call(f32[3,8,32,128]{3,2,1,0:T(8,128)} %vel.1, f32[8,32,128]{2,1,0:T(8,128)} %coef.1, f32[8,32,128]{2,1,0:T(8,128)} %enth.1, ...), custom_call_target="tpu_custom_call" | custom-call | tf_op jit(solution)/shard_map/simple_step/pallas_call | solution.py:701
  29.8 0.9 %finish.1 = (f32[3,8,32,128]{3,2,1,0:T(8,128)}, f32[8,32,128]{2,1,0:T(8,128)}, f32[8,32,128]{2,1,0:T(8,128)}) custom-call(f32[3,8,32,128]{3,2,1,0:T(8,128)S(1)} %get-tuple-element.8.w, f32[3,3,8,32,128]{4,3,2,1,0:T(8,128)S(1)} %get-tuple-element.9.g, f32[3,8,32,128]{3,2,1,0:T(8,128)S(1)} %get-tuple-element.10.u, f32[8,32,128]{2,1,0:T(8,128)S(1)} %get-tuple-element.11.h, ...), custom_call_target="tpu_custom_call" | custom-call | tf_op jit(solution)/shard_map/finish/pallas_call | solution.py:750

commit v5 on v4

--- a/solution.py
+++ b/solution.py
@@ -166,7 +166,7 @@
     vel, coef, enth, void, cells, normal, flag,
     w_out, g_out, u_out, h_out, c_out,
     field, tz, tlo, thi, dz, cx, cy, czm, czp, zlow, av, wc, wn, wf, hot_row, hot_lane, grid,
-    heat, reduce, direct, total, tally, load_sem, copy_sem, send_sem, recv_sem, sum_send, sum_recv, ready,
+    heat, reduce, direct, total, tally, load_sem, copy_sem, send_sem, recv_sem, sum_send, sum_recv, ready, wave,
 ):
     gx, gy, gz = lax.axis_index("gx"), lax.axis_index("gy"), lax.axis_index("gz")
     chip_y, core = gy // 2, lax.rem(gy, 2)
@@ -188,10 +188,23 @@
     def far_first(pairs, n, m):
         return sorted(pairs, key=lambda p: -min(p[0], n - p[0]) - min(p[1], m - p[1]))
 
-    plane = [in_plane(i, j) for i, j in far_first([(i, j) for i in range(NGX) for j in range(NGY // 2) if i or j], NGX, NGY // 2)]
-    column = [in_column(k, j) for k, j in far_first([(k, j) for k in range(NGZ) for j in range(2) if k or j], NGZ, 2)]
+    plane_steps = far_first([(i, j) for i in range(NGX) for j in range(NGY // 2) if i or j], NGX, NGY // 2)
+    column_steps = far_first([(k, j) for k in range(NGZ) for j in range(2) if k or j], NGZ, 2)
+    plane = [in_plane(i, j) for i, j in plane_steps]
+    column = [in_column(k, j) for k, j in column_steps]
 
     inner = (pl.ds(2, BX), pl.ds(8, BY))
+    barrier = pltpu.get_barrier_semaphore()
+    in_root_layer = gz == ROOT[2]
+    in_root_column = (gx == ROOT[0]) & (chip_y == ROOT[1] // 2)
+    is_root = in_root_layer & (gx == ROOT[0]) & (gy == ROOT[1])
+
+    def signal(sem, partners):
+        for partner in partners:
+            pl.semaphore_signal(sem, inc=1, device_id=partner, device_id_type=MESH)
+
+    near = [beside(side) for side in SIDES]
+    signal(barrier, near)
     loads = [
         (cells, wc), (flag, wf), (normal, wn),
         (vel.at[0], field.at[(U0,) + inner]),
@@ -204,10 +217,9 @@
     for copy in loads:
         copy.start()
 
-    barrier = pltpu.get_barrier_semaphore()
-    greeted = [beside(side) for side in SIDES] + plane[::-1] + column[::-1]
-    for partner in greeted:
-        pl.semaphore_signal(barrier, inc=1, device_id=partner, device_id_type=MESH)
+    @pl.when(is_root)
+    def _():
+        signal(barrier, [(x, y, ROOT[2]) for x in range(NGX) for y in range(NGY) if (x, y) != ROOT[:2]])
 
     table = messages(field, tz, tlo, thi, dz)
     copies = [
@@ -356,8 +368,9 @@
     for i, t in ((TB, t_b), (TC, t_c), (TU0, t_u0), (TU1, t_u1), (TU2, t_u2)):
         tz[i] = t
 
-    pl.semaphore_wait(barrier, len(greeted))
+    pl.semaphore_wait(barrier, len(near) + (in_root_layer & jnp.logical_not(is_root)).astype(jnp.int32))
     send(FIRST)
+    signal(wave.at[0], [beside(side) for side in SIDES[:6]])
 
     t_h = None
     half = 0.5 / SCALE
@@ -372,15 +385,9 @@
     tz[TH] = t_h
     send(ENTH)
 
-    in_root_plane = (gz == ROOT[2]) & (core == ROOT[1] % 2)
-    in_root_column = (gx == ROOT[0]) & (chip_y == ROOT[1] // 2)
-    is_root = in_root_plane & in_root_column
-
-    @pl.when(in_root_plane)
-    def _():
-        for partner in column:
-            pl.semaphore_signal(ready, inc=1, device_id=partner, device_id_type=MESH)
-
+    pl.semaphore_wait(wave.at[0], 6)
+    second = [(0, 2, 0), (0, -2, 0), (0, 0, 2), (0, 0, -2)]
+    signal(wave.at[1], [beside(step) for step in second])
 
     def low_high(v):
         return v[0:8], v[8:24], v[24:32]
@@ -391,7 +398,33 @@
         z = z - jnp.where(sub8 == 7, 0.5 * field[f, x + 2, 40:41, :], 0.0)
         return jnp.concatenate([a, m, z], axis=0)
 
+    has_z = jnp.where(low_lane, has[zm_side].astype(jnp.float32), has[zp_side].astype(jnp.float32))
+
+    def z_inside(t):
+        return jnp.where(low_lane, turn(t, -1), turn(t, 1))
+
+    def z_around_x(v, before, after):
+        return (
+            jnp.where(lane8 >= 112, turn(after, -16), turn(v, -16)),
+            jnp.where(lane8 < 16, turn(before, 16), turn(v, 16)),
+        )
+
+    def z_around_y(v, before, after):
+        up = jnp.where(y_group == 3, turn(after, 12), turn(v, -4))
+        down = jnp.where(y_group == 0, turn(before, -12), turn(v, 4))
+        return (
+            turn(jnp.where(sub8 == 0, up, v), -1, 0),
+            turn(jnp.where(sub8 == 7, down, v), 1, 0),
+        )
+
+    zero = jnp.zeros((8, BZ), jnp.float32)
     receive(FIRST)
+    after, before = z_around_x(zero, diagonal(xm_side, 0), diagonal(xp_side, 0))
+    b = pair(tlo[TB], thi[TB]) - 0.5 * (after - before)
+    after, before = z_around_y(zero, diagonal(ym_side, 3), diagonal(yp_side, 3))
+    b = b - 0.5 * (after - before) + jnp.where(low_lane, -0.5, 0.5) * z_inside(tz[TU2])
+    s_w0 = swap(has_z * b)
+
     s_u2 = swap(pair(tlo[TU2], thi[TU2]))
     s_c = swap(pair(tlo[TC], thi[TC]))
     for x in range(BX):
@@ -422,32 +455,6 @@
         b = jnp.where(has[side], b, 0.0)
         for x in range(BX):
             field[W0, x + 2, r : r + 1, :] = b[x : x + 1]
-    has_z = jnp.where(low_lane, has[zm_side].astype(jnp.float32), has[zp_side].astype(jnp.float32))
-
-    def z_inside(t):
-        return jnp.where(low_lane, turn(t, -1), turn(t, 1))
-
-    def z_around_x(v, before, after):
-        return (
-            jnp.where(lane8 >= 112, turn(after, -16), turn(v, -16)),
-            jnp.where(lane8 < 16, turn(before, 16), turn(v, 16)),
-        )
-
-    def z_around_y(v, before, after):
-        up = jnp.where(y_group == 3, turn(after, 12), turn(v, -4))
-        down = jnp.where(y_group == 0, turn(before, -12), turn(v, 4))
-        return (
-            turn(jnp.where(sub8 == 0, up, v), -1, 0),
-            turn(jnp.where(sub8 == 7, down, v), 1, 0),
-        )
-
-    zero = jnp.zeros((8, BZ), jnp.float32)
-    after, before = z_around_x(zero, diagonal(xm_side, 0), diagonal(xp_side, 0))
-    b = pair(tlo[TB], thi[TB]) - 0.5 * (after - before)
-    after, before = z_around_y(zero, diagonal(ym_side, 3), diagonal(yp_side, 3))
-    b = b - 0.5 * (after - before) + jnp.where(low_lane, -0.5, 0.5) * z_inside(tz[TU2])
-    s_w0 = swap(has_z * b)
-
     def operator(f, x, e):
         v = centre(f, x)
         yp, ym = around_y(f, x)
@@ -497,7 +504,52 @@
             low = low + cx[1] * x_edge
         zlow[x] = low
 
+    def face_values(t, qx, qy):
+        lo, hi, own = tlo[t], thi[t], tz[t]
+        v = pair(lo, hi)
+        outer = jnp.where(low_lane, turn(lo, 1), turn(hi, -1))
+        return (
+            (v, outer, z_inside(own))
+            + z_around_x(v, diagonal(xm_side, qx), diagonal(xp_side, qx))
+            + z_around_y(v, diagonal(ym_side, qy), diagonal(yp_side, qy))
+        )
+
+    def row_values(f, q, r, beyond, own, side):
+        v = row_of_field(f, r)
+        after = jnp.where(sub8 == 7, field[f, 10, r : r + 1, :], turn(v, -1, 0))
+        before = jnp.where(sub8 == 0, field[f, 1, r : r + 1, :], turn(v, 1, 0))
+        zp, zm = around_z(v, ends_row(swap(diagonal(side, q)), side[1]))
+        return v, row_of_field(f, beyond), row_of_field(f, own), after, before, zp, zm
+
+    def weights(values, mask):
+        c, *near_c = values
+        return [mask * (half * (c + cn)) for cn in near_c]
+
+    def applied(weight, values):
+        v, *near_v = values
+        terms = [w * (v - vn) for w, vn in zip(weight, near_v)]
+        return ((terms[0] + terms[1]) + (terms[2] + terms[3])) + (terms[4] + terms[5])
+
+    face_weights = weights(face_values(TC, 1, 0), has_z)
+    rows_beyond = ((7, 6, 8, ym_side), (40, 41, 39, yp_side))
+    row_weights = [weights(row_values(C, 0, *at), has[at[3]].astype(jnp.float32)) for at in rows_beyond]
+
+    def image_row(at):
+        out = applied(row_weights[at], row_values(W1, 4, *rows_beyond[at]))
+        r = rows_beyond[at][0]
+        for x in range(BX):
+            field[W2, x + 2, r : r + 1, :] = out[x : x + 1]
+
+    pl.semaphore_wait(wave.at[1], len(second))
+    signal(wave.at[2], [in_plane(i, 0) for i in range(1, NGX)] + [in_column(0, 1)])
+
+    @pl.when(in_root_layer)
+    def _():
+        signal(ready, [in_column(k, 0) for k in range(1, NGZ)])
+
     receive(IMAGE)
+    s_w2 = swap(applied(face_weights, face_values(TW, 4, 4)))
+    image_row(1)
     s_w1 = swap(pair(tlo[TW], thi[TW]))
     for x in range(BX):
         out = operator(W1, x, ends(s_w1, x))
@@ -509,46 +561,7 @@
         out = operator(W1, x, ends(swap(diagonal(side, 4)), inside))
         field[W2, x + 2, ROWS, :] = jnp.where(has[side], out, 0.0)
 
-    def image_row(r, beyond, own, side):
-        sums = []
-        c, v = row_of_field(C, r), row_of_field(W1, r)
-
-        def term(cn, vn):
-            return (c + cn) * (v - vn)
-
-        out = term(row_of_field(C, beyond), row_of_field(W1, beyond)) + term(row_of_field(C, own), row_of_field(W1, own))
-        both = []
-        for f, q, values in ((C, 0, c), (W1, 4, v)):
-            after = jnp.where(sub8 == 7, field[f, 10, r : r + 1, :], turn(values, -1, 0))
-            before = jnp.where(sub8 == 0, field[f, 1, r : r + 1, :], turn(values, 1, 0))
-            zp, zm = around_z(values, ends_row(swap(diagonal(side, q)), side[1]))
-            both.append((after, before, zp, zm))
-        for cn, vn in zip(*both):
-            out = out + term(cn, vn)
-        out = jnp.where(has[side], half * out, 0.0)
-        for x in range(BX):
-            field[W2, x + 2, r : r + 1, :] = out[x : x + 1]
-
-    def image_face():
-        both = []
-        for t, qx, qy in ((TC, 1, 0), (TW, 4, 4)):
-            lo, hi, own = tlo[t], thi[t], tz[t]
-            v = pair(lo, hi)
-            outer = jnp.where(low_lane, turn(lo, 1), turn(hi, -1))
-            both.append(
-                (v, outer, z_inside(own))
-                + z_around_x(v, diagonal(xm_side, qx), diagonal(xp_side, qx))
-                + z_around_y(v, diagonal(ym_side, qy), diagonal(yp_side, qy))
-            )
-        (c, *near_c), (v, *near_v) = both
-        out = zero
-        for cn, vn in zip(near_c, near_v):
-            out = out + (c + cn) * (v - vn)
-        return swap(has_z * (half * out))
-
     image_plane(BX, xp_side, 0)
-    image_row(40, 41, 39, yp_side)
-    s_w2 = image_face()
     for x in range(BX):
         v = centre(W2, x)
         dx = v - centre(W2, x + 1)
@@ -586,15 +599,17 @@
         recv_sem=sum_recv.at[2], device_id=ROOT, device_id_type=MESH,
     )
 
-    @pl.when(jnp.logical_not(in_root_plane))
+    reduce[0, 0:1, :] = row
+    pl.semaphore_wait(wave.at[2], NGX)
+    start_sum(0, plane)
+
+    @pl.when(jnp.logical_not(in_root_layer))
     def _():
         pl.semaphore_wait(ready, 1)
 
-    reduce[0, 0:1, :] = row
     pl.when(jnp.logical_not(is_root))(to_root.start)
-    start_sum(0, plane)
     image_plane(-1, xm_side, 7)
-    image_row(7, 6, 8, ym_side)
+    image_row(0)
     copy_u = pltpu.make_async_copy(field.at[(U0,) + inner], u_out.at[0], copy_sem.at[0])
     copy_u.start()
     copy_v = pltpu.make_async_copy(field.at[(pl.ds(U1, 2),) + inner], u_out.at[pl.ds(1, 2)], copy_sem.at[2])
@@ -739,6 +754,7 @@
             pltpu.SemaphoreType.DMA((3,)),
             pltpu.SemaphoreType.DMA((3,)),
             pltpu.SemaphoreType.REGULAR,
+            pltpu.SemaphoreType.REGULAR((3,)),
         ],
         compiler_params=pltpu.CompilerParams(
             collective_id=0, has_side_effects=True, vmem_limit_bytes=32 * 1024 * 1024

time: 30.8 us -> 29.5 us (0.958)
  the two profiles are of different devices: /device:TPU:2 before, /device:TPU:1 now
where the time goes in v5:
time: 29.5 us; the launch traced here: 29 us
  Pallas kernels  28.4 us (96%)
  between operations  0.64 us (2%)
    pallas_call x1, Pallas kernels, shards(): pl.pallas_call(kernel, out_shape=(jax.ShapeDtypeStruct((3,) + block, f32)...  27.5 us
    pallas_call x1, Pallas kernels, shards(): pl.pallas_call(finish, out_shape=(jax.ShapeDtypeStruct((3,) + block, f32)...  0.87 us

profile of v5, /device:TPU:1, one launch (start us, length us, event | category | flops | bytes accessed | tf_op | source)
XLA Modules:
  0.0 29.0 jit_solution(10817041936183875321)
XLA Ops:
  0.6 27.5 %simple_step.1 = (f32[3,8,32,128]{3,2,1,0:T(8,128)S(1)}, f32[3,3,8,32,128]{4,3,2,1,0:T(8,128)S(1)}, f32[3,8,32,128]{3,2,1,0:T(8,128)S(1)}, f32[8,32,128]{2,1,0:T(8,128)S(1)}, f32[3,8,128]{2,1,0:T(8,128)S(1)}) custom-call(f32[3,8,32,128]{3,2,1,0:T(8,128)} %vel.1, f32[8,32,128]{2,1,0:T(8,128)} %coef.1, f32[8,32,128]{2,1,0:T(8,128)} %enth.1, ...), custom_call_target="tpu_custom_call" | custom-call | tf_op jit(solution)/shard_map/simple_step/pallas_call | solution.py:716
  28.1 0.9 %finish.1 = (f32[3,8,32,128]{3,2,1,0:T(8,128)}, f32[8,32,128]{2,1,0:T(8,128)}, f32[8,32,128]{2,1,0:T(8,128)}) custom-call(f32[3,8,32,128]{3,2,1,0:T(8,128)S(1)} %get-tuple-element.8.w, f32[3,3,8,32,128]{4,3,2,1,0:T(8,128)S(1)} %get-tuple-element.9.g, f32[3,8,32,128]{3,2,1,0:T(8,128)S(1)} %get-tuple-element.10.u, f32[8,32,128]{2,1,0:T(8,128)S(1)} %get-tuple-element.11.h, ...), custom_call_target="tpu_custom_call" | custom-call | tf_op jit(solution)/shard_map/finish/pallas_call | solution.py:766

commit v6 on v5

--- a/solution.py
+++ b/solution.py
@@ -26,7 +26,8 @@
 SIDES = ((-1, 0, 0), (1, 0, 0), (0, -1, 0), (0, 1, 0), (0, 0, -1), (0, 0, 1)) + XY + XZ + YZ
 FIRST, ENTH, IMAGE = range(3)
 PIVOT_FLOOR = 1e-9
-ROOT = (0, 1, 0)
+EARLY_CHIPS = ((0, 0), (1, 0), (3, 0), (2, 0), (0, 1))
+EARLY = tuple((x, 2 * y + c, 0) for x, y in EARLY_CHIPS for c in (1, 0))
 DEVICES = 256
 
 
@@ -195,9 +196,9 @@
 
     inner = (pl.ds(2, BX), pl.ds(8, BY))
     barrier = pltpu.get_barrier_semaphore()
-    in_root_layer = gz == ROOT[2]
-    in_root_column = (gx == ROOT[0]) & (chip_y == ROOT[1] // 2)
-    is_root = in_root_layer & (gx == ROOT[0]) & (gy == ROOT[1])
+    in_layer = gz == 0
+    in_early_column = ((gx == 0) & (chip_y < 2)) | (chip_y == 0)
+    is_early = in_layer & in_early_column
 
     def signal(sem, partners):
         for partner in partners:
@@ -216,10 +217,6 @@
     loads = [pltpu.make_async_copy(s, d, load_sem.at[i]) for i, (s, d) in enumerate(loads)]
     for copy in loads:
         copy.start()
-
-    @pl.when(is_root)
-    def _():
-        signal(barrier, [(x, y, ROOT[2]) for x in range(NGX) for y in range(NGY) if (x, y) != ROOT[:2]])
 
     table = messages(field, tz, tlo, thi, dz)
     copies = [
@@ -368,7 +365,7 @@
     for i, t in ((TB, t_b), (TC, t_c), (TU0, t_u0), (TU1, t_u1), (TU2, t_u2)):
         tz[i] = t
 
-    pl.semaphore_wait(barrier, len(near) + (in_root_layer & jnp.logical_not(is_root)).astype(jnp.int32))
+    pl.semaphore_wait(barrier, len(near))
     send(FIRST)
     signal(wave.at[0], [beside(side) for side in SIDES[:6]])
 
@@ -543,8 +540,9 @@
     pl.semaphore_wait(wave.at[1], len(second))
     signal(wave.at[2], [in_plane(i, 0) for i in range(1, NGX)] + [in_column(0, 1)])
 
-    @pl.when(in_root_layer)
-    def _():
+    @pl.when(in_layer)
+    def _():
+        pl.semaphore_wait(wave.at[2], NGX)
         signal(ready, [in_column(k, 0) for k in range(1, NGZ)])
 
     receive(IMAGE)
@@ -594,20 +592,28 @@
             sum_copy(phase, slot, partner).start()
 
     me = (gx * NGY + gy) * NGZ + gz
-    to_root = pltpu.make_async_remote_copy(
-        src_ref=reduce.at[0, pl.ds(0, 1)], dst_ref=direct.at[me], send_sem=sum_send.at[2],
-        recv_sem=sum_recv.at[2], device_id=ROOT, device_id_type=MESH,
-    )
-
+    to_early = [
+        pltpu.make_async_remote_copy(
+            src_ref=reduce.at[0, pl.ds(0, 1)], dst_ref=direct.at[pl.ds(me, 1)], send_sem=sum_send.at[2],
+            recv_sem=sum_recv.at[2], device_id=device, device_id_type=MESH,
+        )
+        for device in EARLY
+    ]
     reduce[0, 0:1, :] = row
-    pl.semaphore_wait(wave.at[2], NGX)
-    start_sum(0, plane)
-
-    @pl.when(jnp.logical_not(in_root_layer))
-    def _():
+
+    @pl.when(in_layer)
+    def _():
+        start_sum(0, plane)
+
+    @pl.when(jnp.logical_not(in_layer))
+    def _():
+        pl.semaphore_wait(wave.at[2], NGX)
+        start_sum(0, plane)
         pl.semaphore_wait(ready, 1)
 
-    pl.when(jnp.logical_not(is_root))(to_root.start)
+    for device, copy in zip(EARLY, to_early):
+        pl.when((gx != device[0]) | (gy != device[1]) | (gz != device[2]))(copy.start)
+
     image_plane(-1, xm_side, 7)
     image_row(0)
     copy_u = pltpu.make_async_copy(field.at[(U0,) + inner], u_out.at[0], copy_sem.at[0])
@@ -642,24 +648,24 @@
     high, low = row_total(reduce[0])
     reduce[1, 0:1, :] = jnp.where(lane8 < 8, high, turn(low, 8))[0:1]
 
-    @pl.when(jnp.logical_not(in_root_column) | is_root)
+    @pl.when(jnp.logical_not(in_early_column))
     def _():
         start_sum(1, column)
 
-    @pl.when(in_root_column & jnp.logical_not(is_root))
+    @pl.when(in_early_column)
     def _():
         for slot, partner in enumerate(column):
-            pl.when((partner[1] != ROOT[1]) | (partner[2] != ROOT[2]))(sum_copy(1, slot, partner).start)
-
-    @pl.when(is_root)
-    def _():
-        direct[(ROOT[0] * NGY + ROOT[1]) * NGZ + ROOT[2]] = row
+            pl.when(partner[2] != 0)(sum_copy(1, slot, partner).start)
+
+    @pl.when(is_early)
+    def _():
+        direct[pl.ds(me, 1), :] = row
         sum_whole(2, DEVICES - 1).wait_recv()
-        high, low = row_total(direct[...].reshape(DEVICES, BZ))
+        high, low = row_total(direct[...])
         total[0] = high
         total[1] = low
 
-    @pl.when(jnp.logical_not(is_root))
+    @pl.when(jnp.logical_not(is_early))
     def _():
         sum_whole(1, 15).wait_recv()
         high, low = row_total(reduce[1])
@@ -677,15 +683,20 @@
         c_out[i] = v
     sum_whole(0, 15).wait_send()
 
-    @pl.when(in_root_column & jnp.logical_not(is_root))
+    @pl.when(jnp.logical_not(in_early_column))
+    def _():
+        sum_whole(1, 15).wait_send()
+        sum_whole(2, len(EARLY)).wait_send()
+
+    @pl.when(in_early_column & in_layer)
     def _():
         sum_whole(1, 14).wait_send()
-
-    @pl.when(jnp.logical_not(in_root_column) | is_root)
-    def _():
-        sum_whole(1, 15).wait_send()
-
-    pl.when(jnp.logical_not(is_root))(to_root.wait_send)
+        sum_whole(2, len(EARLY) - 1).wait_send()
+
+    @pl.when(in_early_column & jnp.logical_not(in_layer))
+    def _():
+        sum_whole(1, 13).wait_send()
+        sum_whole(2, len(EARLY)).wait_send()
 
 
 def finish(w, g, u, h, c, vel_out, p_out, h_out, vel, p, sem):
@@ -744,7 +755,7 @@
             pltpu.VMEM((BX * BY, BZ), f32),
             pltpu.VMEM(block, f32),
             pltpu.VMEM((2, 16, BZ), f32),
-            pltpu.VMEM((DEVICES, 1, BZ), f32),
+            pltpu.VMEM((DEVICES, BZ), f32),
             pltpu.VMEM((2, 8, BZ), f32),
             pltpu.VMEM((1024, BZ), f32),
             pltpu.SemaphoreType.DMA((8,)),

time: 29.5 us -> 29.3 us (level); the launches traced: 29 us -> 29.1 us
  no operation moved by 1% of the time
where the time goes in v6:
time: 29.3 us; the launch traced here: 29.1 us
  Pallas kernels  28.5 us (97%)
  between operations  0.64 us (2%)
    pallas_call x1, Pallas kernels, shards(): pl.pallas_call(kernel, out_shape=(jax.ShapeDtypeStruct((3,) + block, f32)...  27.6 us
    pallas_call x1, Pallas kernels, shards(): pl.pallas_call(finish, out_shape=(jax.ShapeDtypeStruct((3,) + block, f32)...  0.87 us

profile of v6, /device:TPU:1, one launch (start us, length us, event | category | flops | bytes accessed | tf_op | source)
XLA Modules:
  0.0 29.1 jit_solution(7557203947449453792)
XLA Ops:
  0.6 27.6 %simple_step.1 = (f32[3,8,32,128]{3,2,1,0:T(8,128)S(1)}, f32[3,3,8,32,128]{4,3,2,1,0:T(8,128)S(1)}, f32[3,8,32,128]{3,2,1,0:T(8,128)S(1)}, f32[8,32,128]{2,1,0:T(8,128)S(1)}, f32[3,8,128]{2,1,0:T(8,128)S(1)}) custom-call(f32[3,8,32,128]{3,2,1,0:T(8,128)} %vel.1, f32[8,32,128]{2,1,0:T(8,128)} %coef.1, f32[8,32,128]{2,1,0:T(8,128)} %enth.1, ...), custom_call_target="tpu_custom_call" | custom-call | tf_op jit(solution)/shard_map/simple_step/pallas_call | solution.py:727
  28.3 0.9 %finish.1 = (f32[3,8,32,128]{3,2,1,0:T(8,128)}, f32[8,32,128]{2,1,0:T(8,128)}, f32[8,32,128]{2,1,0:T(8,128)}) custom-call(f32[3,8,32,128]{3,2,1,0:T(8,128)S(1)} %get-tuple-element.8.w, f32[3,3,8,32,128]{4,3,2,1,0:T(8,128)S(1)} %get-tuple-element.9.g, f32[3,8,32,128]{3,2,1,0:T(8,128)S(1)} %get-tuple-element.10.u, f32[8,32,128]{2,1,0:T(8,128)S(1)} %get-tuple-element.11.h, ...), custom_call_target="tpu_custom_call" | custom-call | tf_op jit(solution)/shard_map/finish/pallas_call | solution.py:777

commit v7 on v6

--- a/solution.py
+++ b/solution.py
@@ -17,14 +17,14 @@
 SCALE = 16.0
 H, C, U0, BP, U1, U2, W0, W1, W2 = range(9)
 FIELDS = 9
-TU0, TC, TU2, TB, TU1, TH, TW = range(7)
+TU0, TU2, TU1, TB, TC, TH, TW = range(7)
 ROWS = slice(8, 40)
 SIGNS = (-1, 1)
 XZ = tuple((a, 0, c) for a in SIGNS for c in SIGNS)
 YZ = tuple((0, b, c) for b in SIGNS for c in SIGNS)
 XY = tuple((a, b, 0) for a in SIGNS for b in SIGNS)
 SIDES = ((-1, 0, 0), (1, 0, 0), (0, -1, 0), (0, 1, 0), (0, 0, -1), (0, 0, 1)) + XY + XZ + YZ
-FIRST, ENTH, IMAGE = range(3)
+FIRST, OUTER, ENTH, IMAGE = range(4)
 PIVOT_FLOOR = 1e-9
 EARLY_CHIPS = ((0, 0), (1, 0), (3, 0), (2, 0), (0, 1))
 EARLY = tuple((x, 2 * y + c, 0) for x, y in EARLY_CHIPS for c in (1, 0))
@@ -121,30 +121,32 @@
 
 def messages(field, tz, tlo, thi, dz):
     xs, xd = {-1: 2, 1: 9}, {-1: 10, 1: 1}
+    xs1, xd1 = {-1: 3, 1: 8}, {-1: 11, 1: 0}
     ys, yd = {-1: 8, 1: 39}, {-1: 40, 1: 7}
     xs2, xd2 = {-1: pl.ds(2, 2), 1: pl.ds(8, 2)}, {-1: pl.ds(10, 2), 1: pl.ds(0, 2)}
     ys2, yd2 = {-1: pl.ds(8, 2), 1: pl.ds(38, 2)}, {-1: pl.ds(40, 2), 1: pl.ds(6, 2)}
     rows, planes = pl.ds(8, BY), pl.ds(2, BX)
-    table = [[], [], []]
+    table = [[], [], [], []]
     for side in XZ + YZ + XY + SIDES[:2] + SIDES[4:6] + SIDES[2:4]:
         a, b, c = side
         far = thi if c < 0 else tlo
         slot = (XZ + YZ).index(opposite(side)) if side in XZ + YZ else None
-        enth = []
+        enth = outer = []
         if side in XZ:
-            first = [(tz.at[pl.ds(TU0, 3)], dz.at[slot, pl.ds(0, 3)])]
+            first = [(tz.at[pl.ds(TU0, 2)], dz.at[slot, pl.ds(0, 2)])]
+            outer = [(tz.at[TC], dz.at[slot, 2])]
             image = [(tz.at[TW], dz.at[slot, 4])]
         elif side in YZ:
-            first = [(tz.at[pl.ds(TC, 4)], dz.at[slot, pl.ds(0, 4)])]
+            first = [(tz.at[pl.ds(TU2, 2)], dz.at[slot, pl.ds(0, 2)])]
+            outer = [(tz.at[TC], dz.at[slot, 2])]
             image = [(tz.at[TW], dz.at[slot, 4])]
         elif side in XY:
-            first = [(field.at[pl.ds(C, 4), xs[a], ys[b]], field.at[pl.ds(C, 4), xd[a], yd[b]])]
+            first = [(field.at[pl.ds(U0, 3), xs[a], ys[b]], field.at[pl.ds(U0, 3), xd[a], yd[b]])]
+            outer = [(field.at[C, xs[a], ys[b]], field.at[C, xd[a], yd[b]])]
             image = [(field.at[W1, xs[a], ys[b]], field.at[W1, xd[a], yd[b]])]
         elif a:
-            first = [
-                (field.at[C, xs2[a], rows], field.at[C, xd2[a], rows]),
-                (field.at[pl.ds(U0, 2), xs[a], rows], field.at[pl.ds(U0, 2), xd[a], rows]),
-            ]
+            first = [(field.at[pl.ds(C, 3), xs[a], rows], field.at[pl.ds(C, 3), xd[a], rows])]
+            outer = [(field.at[C, xs1[a], rows], field.at[C, xd1[a], rows])]
             enth = [(field.at[H, xs[a], rows], field.at[H, xd[a], rows])]
             image = [(field.at[W1, xs2[a], rows], field.at[W1, xd2[a], rows])]
         elif b:
@@ -155,10 +157,10 @@
             enth = [(field.at[H, planes, ys[b]], field.at[H, planes, yd[b]])]
             image = [(field.at[W1, planes, ys2[b]], field.at[W1, planes, yd2[b]])]
         else:
-            first = [(tz.at[pl.ds(TC, 3)], far.at[pl.ds(TC, 3)])]
+            first = [(tz.at[pl.ds(TU2, 4)], far.at[pl.ds(TU2, 4)])]
             enth = [(tz.at[TH], far.at[TH])]
             image = [(tz.at[TW], far.at[TW])]
-        for kind, pairs in ((FIRST, first), (ENTH, enth), (IMAGE, image)):
+        for kind, pairs in ((FIRST, first), (OUTER, outer), (ENTH, enth), (IMAGE, image)):
             table[kind] += [(side, src, dst) for src, dst in pairs]
     return table
 
@@ -204,7 +206,7 @@
         for partner in partners:
             pl.semaphore_signal(sem, inc=1, device_id=partner, device_id_type=MESH)
 
-    near = [beside(side) for side in SIDES]
+    near = [beside(side) for side in XZ + YZ + XY + SIDES[4:6] + SIDES[:4]]
     signal(barrier, near)
     loads = [
         (cells, wc), (flag, wf), (normal, wn),
@@ -218,6 +220,12 @@
     for copy in loads:
         copy.start()
 
+    for device in EARLY:
+
+        @pl.when((gx == device[0]) & (gy == device[1]) & in_layer)
+        def _():
+            signal(barrier, [(x, y, 0) for x in range(NGX) for y in range(NGY) if (x, y) != device[:2]])
+
     table = messages(field, tz, tlo, thi, dz)
     copies = [
         [
@@ -227,7 +235,7 @@
             )
             for side, src, dst in table[kind]
         ]
-        for kind in range(3)
+        for kind in range(4)
     ]
 
     def whole(kind):
@@ -365,9 +373,12 @@
     for i, t in ((TB, t_b), (TC, t_c), (TU0, t_u0), (TU1, t_u1), (TU2, t_u2)):
         tz[i] = t
 
-    pl.semaphore_wait(barrier, len(near))
+    greeters = jnp.where(in_layer, len(EARLY) - is_early.astype(jnp.int32), 0)
+    pl.semaphore_wait(barrier, len(near) + greeters)
     send(FIRST)
-    signal(wave.at[0], [beside(side) for side in SIDES[:6]])
+    send(OUTER)
+    signal(wave.at[0], [beside(side) for side in SIDES[:4]])
+    signal(wave.at[3], [beside(side) for side in SIDES[4:6]])
 
     t_h = None
     half = 0.5 / SCALE
@@ -382,9 +393,10 @@
     tz[TH] = t_h
     send(ENTH)
 
-    pl.semaphore_wait(wave.at[0], 6)
-    second = [(0, 2, 0), (0, -2, 0), (0, 0, 2), (0, 0, -2)]
-    signal(wave.at[1], [beside(step) for step in second])
+    pl.semaphore_wait(wave.at[0], 4)
+    signal(wave.at[1], [beside((0, 2, 0)), beside((0, -2, 0))])
+    pl.semaphore_wait(wave.at[3], 2)
+    signal(wave.at[4], [beside((0, 0, 2)), beside((0, 0, -2))])
 
     def low_high(v):
         return v[0:8], v[8:24], v[24:32]
@@ -418,7 +430,7 @@
     receive(FIRST)
     after, before = z_around_x(zero, diagonal(xm_side, 0), diagonal(xp_side, 0))
     b = pair(tlo[TB], thi[TB]) - 0.5 * (after - before)
-    after, before = z_around_y(zero, diagonal(ym_side, 3), diagonal(yp_side, 3))
+    after, before = z_around_y(zero, diagonal(ym_side, 1), diagonal(yp_side, 1))
     b = b - 0.5 * (after - before) + jnp.where(low_lane, -0.5, 0.5) * z_inside(tz[TU2])
     s_w0 = swap(has_z * b)
 
@@ -442,13 +454,13 @@
     cx[9] = half * (centre(C, 7) + centre(C, 8))
     for x, own, sign, side, inside in ((-1, 0, -0.5, xm_side, 7), (BX, BX - 1, 0.5, xp_side, 0)):
         b = centre(BP, x) + sign * centre(U0, own)
-        b = y_ends(b, U1, x) + ends_half32 * ends(swap(diagonal(side, 2)), inside)
+        b = y_ends(b, U1, x) + ends_half32 * ends(swap(diagonal(side, 1)), inside)
         field[W0, x + 2, ROWS, :] = jnp.where(has[side], b, 0.0)
     for r, own, sign, side in ((7, 8, -0.5, ym_side), (40, 39, 0.5, yp_side)):
         b = row_of_field(BP, r) + sign * row_of_field(U1, own)
         b = b + jnp.where(sub8 == 0, 0.5 * field[U0, 1, r : r + 1, :], 0.0)
         b = b - jnp.where(sub8 == 7, 0.5 * field[U0, 10, r : r + 1, :], 0.0)
-        b = b + ends_half * ends_row(swap(diagonal(side, 1)), side[1])
+        b = b + ends_half * ends_row(swap(diagonal(side, 0)), side[1])
         b = jnp.where(has[side], b, 0.0)
         for x in range(BX):
             field[W0, x + 2, r : r + 1, :] = b[x : x + 1]
@@ -467,6 +479,14 @@
         t_w = pack(out, t_w, x)
     tz[TW] = t_w
     send(IMAGE)
+    pl.semaphore_wait(wave.at[1], 2)
+    signal(wave.at[2], [in_plane(i, 0) for i in range(1, NGX)])
+
+    @pl.when(in_layer)
+    def _():
+        pl.semaphore_wait(wave.at[4], 2)
+        signal(ready, [in_column(k, 0) for k in range(1, NGZ)])
+
 
     def fold(v):
         return (v[0:8] + v[8:16]) + (v[16:24] + v[24:32])
@@ -479,6 +499,7 @@
     for x in range(BX):
         v, out = centre(W0, x), centre(W1, x)
         m[0], m[1], m[2] = plus(m[0], v * v), plus(m[1], v * out), plus(m[2], out * out)
+    receive(OUTER)
     for x, side, inside in ((-1, xm_side, 7), (BX, xp_side, 0)):
         c = centre(C, x)
         if x < 0:
@@ -488,7 +509,7 @@
         after, before = around_y(C, x)
         cy[x + 1, 0:32] = half * (c + before)
         cy[x + 1, 32:33] = half * (c[31:32] + after[31:32])
-        after, before = around_z(c, ends(swap(diagonal(side, 1)), inside))
+        after, before = around_z(c, ends(swap(diagonal(side, 2)), inside))
         czp[x + 1] = half * (c + after)
         czm[x + 1] = half * (c + before)
     z_edge = jnp.where(has[zm_side], 0.0, 1.0)
@@ -527,9 +548,9 @@
         terms = [w * (v - vn) for w, vn in zip(weight, near_v)]
         return ((terms[0] + terms[1]) + (terms[2] + terms[3])) + (terms[4] + terms[5])
 
-    face_weights = weights(face_values(TC, 1, 0), has_z)
+    face_weights = weights(face_values(TC, 2, 2), has_z)
     rows_beyond = ((7, 6, 8, ym_side), (40, 41, 39, yp_side))
-    row_weights = [weights(row_values(C, 0, *at), has[at[3]].astype(jnp.float32)) for at in rows_beyond]
+    row_weights = [weights(row_values(C, 2, *at), has[at[3]].astype(jnp.float32)) for at in rows_beyond]
 
     def image_row(at):
         out = applied(row_weights[at], row_values(W1, 4, *rows_beyond[at]))
@@ -537,13 +558,6 @@
         for x in range(BX):
             field[W2, x + 2, r : r + 1, :] = out[x : x + 1]
 
-    pl.semaphore_wait(wave.at[1], len(second))
-    signal(wave.at[2], [in_plane(i, 0) for i in range(1, NGX)] + [in_column(0, 1)])
-
-    @pl.when(in_layer)
-    def _():
-        pl.semaphore_wait(wave.at[2], NGX)
-        signal(ready, [in_column(k, 0) for k in range(1, NGZ)])
 
     receive(IMAGE)
     s_w2 = swap(applied(face_weights, face_values(TW, 4, 4)))
@@ -601,18 +615,17 @@
     ]
     reduce[0, 0:1, :] = row
 
-    @pl.when(in_layer)
-    def _():
-        start_sum(0, plane)
+    pl.semaphore_wait(wave.at[2], NGX - 1)
+    start_sum(0, plane)
 
     @pl.when(jnp.logical_not(in_layer))
     def _():
-        pl.semaphore_wait(wave.at[2], NGX)
-        start_sum(0, plane)
+        pl.semaphore_wait(wave.at[4], 2)
         pl.semaphore_wait(ready, 1)
 
     for device, copy in zip(EARLY, to_early):
         pl.when((gx != device[0]) | (gy != device[1]) | (gz != device[2]))(copy.start)
+    signal(wave.at[5], [in_column(0, 1)])
 
     image_plane(-1, xm_side, 7)
     image_row(0)
@@ -641,9 +654,10 @@
     copy_u.wait()
     copy_v.wait()
     copy_w.wait()
-    for kind in range(3):
+    for kind in range(4):
         whole(kind).wait_send()
 
+    pl.semaphore_wait(wave.at[5], 1)
     sum_whole(0, 15).wait_recv()
     high, low = row_total(reduce[0])
     reduce[1, 0:1, :] = jnp.where(lane8 < 8, high, turn(low, 8))[0:1]
@@ -760,12 +774,12 @@
             pltpu.VMEM((1024, BZ), f32),
             pltpu.SemaphoreType.DMA((8,)),
             pltpu.SemaphoreType.DMA((3,)),
-            pltpu.SemaphoreType.DMA((3,)),
-            pltpu.SemaphoreType.DMA((3,)),
+            pltpu.SemaphoreType.DMA((4,)),
+            pltpu.SemaphoreType.DMA((4,)),
             pltpu.SemaphoreType.DMA((3,)),
             pltpu.SemaphoreType.DMA((3,)),
             pltpu.SemaphoreType.REGULAR,
-            pltpu.SemaphoreType.REGULAR((3,)),
+            pltpu.SemaphoreType.REGULAR((6,)),
         ],
         compiler_params=pltpu.CompilerParams(
             collective_id=0, has_side_effects=True, vmem_limit_bytes=32 * 1024 * 1024

time: 29.3 us -> 28.6 us (0.976)
  Pallas kernels: 28.5 us -> 27.9 us
    pallas_call x1, Pallas kernels: 27.6 us -> 27 us  [shards(): pl.pallas_call(kernel, out_shape=(jax.ShapeDtypeStruct((3,) + block, f32)...]
where the time goes in v7:
time: 28.6 us; the launch traced here: 28.5 us
  Pallas kernels  27.9 us (98%)
  between operations  0.64 us (2%)
    pallas_call x1, Pallas kernels, shards(): pl.pallas_call(kernel, out_shape=(jax.ShapeDtypeStruct((3,) + block, f32)...  27 us
    pallas_call x1, Pallas kernels, shards(): pl.pallas_call(finish, out_shape=(jax.ShapeDtypeStruct((3,) + block, f32)...  0.87 us

profile of v7, /device:TPU:1, one launch (start us, length us, event | category | flops | bytes accessed | tf_op | source)
XLA Modules:
  0.0 28.5 jit_solution(9760749599333295578)
XLA Ops:
  0.6 27.0 %simple_step.1 = (f32[3,8,32,128]{3,2,1,0:T(8,128)S(1)}, f32[3,3,8,32,128]{4,3,2,1,0:T(8,128)S(1)}, f32[3,8,32,128]{3,2,1,0:T(8,128)S(1)}, f32[8,32,128]{2,1,0:T(8,128)S(1)}, f32[3,8,128]{2,1,0:T(8,128)S(1)}) custom-call(f32[3,8,32,128]{3,2,1,0:T(8,128)} %vel.1, f32[8,32,128]{2,1,0:T(8,128)} %coef.1, f32[8,32,128]{2,1,0:T(8,128)} %enth.1, ...), custom_call_target="tpu_custom_call" | custom-call | tf_op jit(solution)/shard_map/simple_step/pallas_call | solution.py:741
  27.6 0.9 %finish.1 = (f32[3,8,32,128]{3,2,1,0:T(8,128)}, f32[8,32,128]{2,1,0:T(8,128)}, f32[8,32,128]{2,1,0:T(8,128)}) custom-call(f32[3,8,32,128]{3,2,1,0:T(8,128)S(1)} %get-tuple-element.8.w, f32[3,3,8,32,128]{4,3,2,1,0:T(8,128)S(1)} %get-tuple-element.9.g, f32[3,8,32,128]{3,2,1,0:T(8,128)S(1)} %get-tuple-element.10.u, f32[8,32,128]{2,1,0:T(8,128)S(1)} %get-tuple-element.11.h, ...), custom_call_target="tpu_custom_call" | custom-call | tf_op jit(solution)/shard_map/finish/pallas_call | solution.py:791

commit v8 on v7

--- a/solution.py
+++ b/solution.py
@@ -434,6 +434,18 @@
     b = b - 0.5 * (after - before) + jnp.where(low_lane, -0.5, 0.5) * z_inside(tz[TU2])
     s_w0 = swap(has_z * b)
 
+    for x, own, sign, side, inside in ((-1, 0, -0.5, xm_side, 7), (BX, BX - 1, 0.5, xp_side, 0)):
+        b = centre(BP, x) + sign * centre(U0, own)
+        b = y_ends(b, U1, x) + ends_half32 * ends(swap(diagonal(side, 1)), inside)
+        field[W0, x + 2, ROWS, :] = jnp.where(has[side], b, 0.0)
+    for r, own, sign, side in ((7, 8, -0.5, ym_side), (40, 39, 0.5, yp_side)):
+        b = row_of_field(BP, r) + sign * row_of_field(U1, own)
+        b = b + jnp.where(sub8 == 0, 0.5 * field[U0, 1, r : r + 1, :], 0.0)
+        b = b - jnp.where(sub8 == 7, 0.5 * field[U0, 10, r : r + 1, :], 0.0)
+        b = b + ends_half * ends_row(swap(diagonal(side, 0)), side[1])
+        b = jnp.where(has[side], b, 0.0)
+        for x in range(BX):
+            field[W0, x + 2, r : r + 1, :] = b[x : x + 1]
     s_u2 = swap(pair(tlo[TU2], thi[TU2]))
     s_c = swap(pair(tlo[TC], thi[TC]))
     for x in range(BX):
@@ -452,18 +464,6 @@
         cy[x + 1, 32:33] = half * (c[31:32] + field[C, x + 2, 40:41, :])
     cx[1] = half * (centre(C, 0) + centre(C, -1))
     cx[9] = half * (centre(C, 7) + centre(C, 8))
-    for x, own, sign, side, inside in ((-1, 0, -0.5, xm_side, 7), (BX, BX - 1, 0.5, xp_side, 0)):
-        b = centre(BP, x) + sign * centre(U0, own)
-        b = y_ends(b, U1, x) + ends_half32 * ends(swap(diagonal(side, 1)), inside)
-        field[W0, x + 2, ROWS, :] = jnp.where(has[side], b, 0.0)
-    for r, own, sign, side in ((7, 8, -0.5, ym_side), (40, 39, 0.5, yp_side)):
-        b = row_of_field(BP, r) + sign * row_of_field(U1, own)
-        b = b + jnp.where(sub8 == 0, 0.5 * field[U0, 1, r : r + 1, :], 0.0)
-        b = b - jnp.where(sub8 == 7, 0.5 * field[U0, 10, r : r + 1, :], 0.0)
-        b = b + ends_half * ends_row(swap(diagonal(side, 0)), side[1])
-        b = jnp.where(has[side], b, 0.0)
-        for x in range(BX):
-            field[W0, x + 2, r : r + 1, :] = b[x : x + 1]
     def operator(f, x, e):
         v = centre(f, x)
         yp, ym = around_y(f, x)

time: 28.6 us -> 28.6 us (level)
  no operation moved by 1% of the time
where the time goes in v8:
time: 28.6 us; the launch traced here: 28.5 us
  Pallas kernels  27.9 us (98%)
  between operations  0.64 us (2%)
    pallas_call x1, Pallas kernels, shards(): pl.pallas_call(kernel, out_shape=(jax.ShapeDtypeStruct((3,) + block, f32)...  27 us
    pallas_call x1, Pallas kernels, shards(): pl.pallas_call(finish, out_shape=(jax.ShapeDtypeStruct((3,) + block, f32)...  0.87 us

profile of v8, /device:TPU:1, one launch (start us, length us, event | category | flops | bytes accessed | tf_op | source)
XLA Modules:
  0.0 28.5 jit_solution(10961331780797760357)
XLA Ops:
  0.6 27.0 %simple_step.1 = (f32[3,8,32,128]{3,2,1,0:T(8,128)S(1)}, f32[3,3,8,32,128]{4,3,2,1,0:T(8,128)S(1)}, f32[3,8,32,128]{3,2,1,0:T(8,128)S(1)}, f32[8,32,128]{2,1,0:T(8,128)S(1)}, f32[3,8,128]{2,1,0:T(8,128)S(1)}) custom-call(f32[3,8,32,128]{3,2,1,0:T(8,128)} %vel.1, f32[8,32,128]{2,1,0:T(8,128)} %coef.1, f32[8,32,128]{2,1,0:T(8,128)} %enth.1, ...), custom_call_target="tpu_custom_call" | custom-call | tf_op jit(solution)/shard_map/simple_step/pallas_call | solution.py:741
  27.6 0.9 %finish.1 = (f32[3,8,32,128]{3,2,1,0:T(8,128)}, f32[8,32,128]{2,1,0:T(8,128)}, f32[8,32,128]{2,1,0:T(8,128)}) custom-call(f32[3,8,32,128]{3,2,1,0:T(8,128)S(1)} %get-tuple-element.8.w, f32[3,3,8,32,128]{4,3,2,1,0:T(8,128)S(1)} %get-tuple-element.9.g, f32[3,8,32,128]{3,2,1,0:T(8,128)S(1)} %get-tuple-element.10.u, f32[8,32,128]{2,1,0:T(8,128)S(1)} %get-tuple-element.11.h, ...), custom_call_target="tpu_custom_call" | custom-call | tf_op jit(solution)/shard_map/finish/pallas_call | solution.py:791
